TPU v7x, 32 devices: a whole 2x2x4 slice. The times are simulated.
32 devices in a mesh: seq: 16 (over z, x, core), head: 2 (over y).
Axes of the slice: x: 2, y: 2, z: 4, core: 2. Of those that a mesh axis runs over, the one named last changes fastest.
Arguments:
- queries: bfloat16 [8192, 8192], P(('seq', 'head')), may hold values from -9 to 9
- keys: bfloat16 [8192, 1024], P(('seq', 'head')), may hold values from -9 to 9
- values: bfloat16 [8192, 1024], P(('seq', 'head')), may hold values from -6 to 6
- prefix_keys: bfloat16 [32768, 1024], P('seq', 'head'), may hold values from -6 to 6
- prefix_values: bfloat16 [32768, 1024], P('seq', 'head'), may hold values from -6 to 6
- roles: int32 [64], P('head'), may hold values from 0 to 1, as said below
- columns: int32 [64, 6], P('head'), may hold values from 0 to 479, as said below
- col_count: int32 [64], P('head'), may hold values from 1 to 6, as said below
- diagonals: int32 [64, 4], P('head'), may hold values from 0 to 7, as said below
Outputs:
- attended: bfloat16 [8192, 8192], P('seq', 'head')
Inputs may be any that keep to these rules, and one draw needn't show every extreme that they name: `roles`: 1 marks a retrieval head, 0 a passing head; at most 4 retrieval heads share one key-value head, and some key-value head has exactly 4. `columns`: prefix block indices, blocks of 64 cache rows, distinct within a head. `col_count`: some retrieval head uses all 6 of its column blocks. `diagonals`: distinct within a head; the first offset of every head is 0.
All inputs are finite; a program needn't handle non-finite values.
Results may differ from a plain program's by a relative error of at most 0.0049.
Values may be sent and summed in bfloat16 or wider, within the bound.
A program may use at most 128 MiB of HBM per device.

v0:
```python
import functools
import math

import jax
import jax.numpy as jnp
from jax import lax
from jax.experimental import pallas as pl
from jax.experimental.pallas import tpu as pltpu
from jax.sharding import PartitionSpec as P

QUERY_HEADS = 64
KEY_VALUE_HEADS = 8
SHARE = QUERY_HEADS // KEY_VALUE_HEADS
D = 128
SINK = 128
WIN = 512
BLK = 64
VB = 6
NSL = 4
MAX_RETRIEVERS = 4
QB = 128
SCALE = math.log2(math.e) / math.sqrt(D)
VMEM_LIMIT = 40 * 1024 * 1024


def dot_nt(a, b):
    return lax.dot_general(a, b, (((1,), (1,)), ((), ())), preferred_element_type=jnp.float32)


def dot(a, b):
    return jnp.dot(a, b, preferred_element_type=jnp.float32)


def collect_kernel(own, blk, kv_of, pk, pv, out, sem, sink_sem):
    count = kv_of.shape[0]
    kv_count = pk.shape[1] // D
    out[...] = jnp.zeros_like(out)

    def copies(t):
        rows = pl.ds(pl.multiple_of(blk[t] * BLK, BLK), BLK)
        cols = pl.ds(pl.multiple_of(kv_of[t] * D, D), D)
        first = pl.ds(pl.multiple_of(t * BLK, BLK), BLK)
        second = pl.ds(pl.multiple_of((count + t) * BLK, BLK), BLK)
        return (
            pltpu.make_async_copy(pk.at[rows, cols], out.at[first, :], sem.at[0, t]),
            pltpu.make_async_copy(pv.at[rows, cols], out.at[second, :], sem.at[1, t]),
        )

    def sinks():
        base = 2 * count * BLK
        return [
            pltpu.make_async_copy(
                ref.at[pl.ds(0, SINK), pl.ds(g * D, D)],
                out.at[pl.ds(base + (part * kv_count + g) * SINK, SINK), :],
                sink_sem.at[part, g],
            )
            for part, ref in enumerate((pk, pv))
            for g in range(kv_count)
        ]

    def start(t, carry):
        @pl.when(own[t] == 1)
        def _():
            for copy in copies(t):
                copy.start()

        return carry

    def finish(t, carry):
        @pl.when(own[t] == 1)
        def _():
            for copy in copies(t):
                copy.wait()

        return carry

    @pl.when(own[count] == 1)
    def _():
        for copy in sinks():
            copy.start()

    lax.fori_loop(0, count, start, 0)
    lax.fori_loop(0, count, finish, 0)

    @pl.when(own[count] == 1)
    def _():
        for copy in sinks():
            copy.wait()


def collect(own, blk, kv_of, prefix_keys, prefix_values, rows):
    count = kv_of.shape[0]
    kv_count = prefix_keys.shape[1] // D
    return pl.pallas_call(
        collect_kernel,
        grid_spec=pltpu.PrefetchScalarGridSpec(
            num_scalar_prefetch=3,
            grid=(1,),
            in_specs=[pl.BlockSpec(memory_space=pl.ANY)] * 2,
            out_specs=pl.BlockSpec((rows, D), lambda i, *_: (0, 0)),
            scratch_shapes=[
                pltpu.SemaphoreType.DMA((2, count)),
                pltpu.SemaphoreType.DMA((2, kv_count)),
            ],
        ),
        out_shape=jax.ShapeDtypeStruct((rows, D), jnp.bfloat16),
        compiler_params=pltpu.CompilerParams(vmem_limit_bytes=VMEM_LIMIT),
        name="collect_columns",
    )(own, blk, kv_of, prefix_keys, prefix_values)


def share_kernel(size, orders, mine, out, acc, landed, send_sem, recv_sem):
    me = lax.axis_index("seq")
    bits = len(orders[0])
    barrier = pltpu.get_barrier_semaphore()

    def bit_of(b):
        return lax.rem(me // (1 << b), 2)

    def partner(b):
        return me + (1 - 2 * bit_of(b)) * (1 << b)

    for b in range(bits):
        pl.semaphore_signal(
            barrier, inc=1, device_id={"seq": partner(b)}, device_id_type=pl.DeviceIdType.MESH
        )
    pl.semaphore_wait(barrier, bits)

    streams = len(orders)
    part = mine.shape[0] // streams
    low = [part * w for w in range(streams)]
    length = [part] * streams
    started = {}

    def at(start, n):
        return pl.ds(pl.multiple_of(start, 16), n)

    def move(src, dst, w, step, b):
        copy = pltpu.make_async_remote_copy(
            src_ref=src,
            dst_ref=dst,
            send_sem=send_sem.at[w, step],
            recv_sem=recv_sem.at[w, step],
            device_id={"seq": partner(b)},
            device_id_type=pl.DeviceIdType.MESH,
        )
        copy.start()
        started[w, step] = copy

    def halve(w, step):
        b = orders[w][step]
        half = length[w] // 2
        source = mine if step == 0 else acc
        other = low[w] + (1 - bit_of(b)) * half
        place = part * w + part - length[w]
        move(source.at[at(other, half), :], landed.at[pl.ds(place, half), :], w, step, b)

    def add(w, step):
        b = orders[w][step]
        half = length[w] // 2
        source = mine if step == 0 else acc
        place = part * w + part - length[w]
        keep = at(low[w] + bit_of(b) * half, half)
        started[w, step].wait()
        into = out if step == bits - 1 else acc
        into[keep, :] = source[keep, :] + landed[pl.ds(place, half), :]
        low[w] = low[w] + bit_of(b) * half
        length[w] = half

    def double(w, step):
        b = orders[w][2 * bits - 1 - step]
        whole = out.at[at(low[w], length[w]), :]
        move(whole, whole, w, step, b)

    def join(w, step):
        b = orders[w][2 * bits - 1 - step]
        started[w, step].wait()
        low[w] = low[w] - bit_of(b) * length[w]
        length[w] = 2 * length[w]

    for step in range(2 * bits + 1):
        for w in range(streams):
            if 0 < step <= bits:
                add(w, step - 1)
            elif step > bits:
                join(w, step - 1)
            if step < bits:
                halve(w, step)
            elif step < 2 * bits:
                double(w, step)


def share(mine):
    size = lax.axis_size("seq")
    bits = size.bit_length() - 1
    orders = [list(range(bits)), [0, *range(2, bits), 1]]
    rows = mine.shape[0]
    return pl.pallas_call(
        functools.partial(share_kernel, size, orders),
        out_shape=jax.ShapeDtypeStruct(mine.shape, mine.dtype),
        in_specs=[pl.BlockSpec(memory_space=pltpu.VMEM)],
        out_specs=pl.BlockSpec(memory_space=pltpu.VMEM),
        scratch_shapes=[
            pltpu.VMEM((rows, D), mine.dtype),
            pltpu.VMEM((rows, D), mine.dtype),
            pltpu.SemaphoreType.DMA((len(orders), 2 * bits)),
            pltpu.SemaphoreType.DMA((len(orders), 2 * bits)),
        ],
        compiler_params=pltpu.CompilerParams(
            collective_id=0, has_side_effects=True, vmem_limit_bytes=VMEM_LIMIT
        ),
        cost_estimate=pl.CostEstimate(
            flops=10**10, bytes_accessed=8 * rows * D, transcendentals=0
        ),
        name="share_columns",
    )(mine)


def new_group(heads, i):
    before = heads[jnp.maximum(i - 1, 0)]
    return (i == 0) | (heads[i] // SHARE != before // SHARE)


def passing_kernel(heads, used, q, k, v, pk, pv, sk, sv, out, keys_t, vals):
    i = pl.program_id(0)
    rows = q.shape[0]

    @pl.when(new_group(heads, i))
    def _():
        keys_t[:, :SINK] = sk[...].T
        keys_t[:, SINK : SINK + WIN] = pk[...].T
        keys_t[:, SINK + WIN :] = k[...].T
        vals[:SINK, :D] = sv[...]
        vals[SINK : SINK + WIN, :D] = pv[...]
        vals[SINK + WIN :, :D] = v[...]
        vals[:, D:] = jnp.ones_like(vals[:, D:])

    @pl.when(i < used[0])
    def _():
        row = lax.broadcasted_iota(jnp.int32, (QB, QB), 0)
        col = lax.broadcasted_iota(jnp.int32, (QB, QB), 1)
        for r in range(0, rows, QB):
            low, high = SINK + r, SINK + r + WIN + QB
            window = jnp.concatenate([keys_t[:, :SINK], keys_t[:, low:high]], 1)
            s = dot(q[r : r + QB, :], window)
            s = jnp.concatenate(
                [
                    s[:, :SINK],
                    jnp.where(col > row, s[:, SINK : SINK + QB], -jnp.inf),
                    s[:, SINK + QB : SINK + WIN],
                    jnp.where(col <= row, s[:, SINK + WIN :], -jnp.inf),
                ],
                1,
            )
            top = jnp.max(s, axis=1, keepdims=True)
            p = jnp.exp2((s - top) * SCALE).astype(jnp.bfloat16)
            acc = dot(p, jnp.concatenate([vals[:SINK, :], vals[low:high, :]], 0))
            out[r : r + QB, :] = (acc[:, :D] / acc[:, D:]).astype(out.dtype)


def passing(heads, used, q, kv, previous, shared, sink_block):
    rows, width = q.shape
    kv_count = kv.shape[1] // (2 * D)

    def sink_key(i, heads, used):
        return (sink_block + heads[i] // SHARE, 0)

    def sink_value(i, heads, used):
        return (sink_block + kv_count + heads[i] // SHARE, 0)

    def head(i, heads, used):
        return (0, heads[i])

    def key(i, heads, used):
        return (0, heads[i] // SHARE)

    def value(i, heads, used):
        return (0, kv_count + heads[i] // SHARE)

    return pl.pallas_call(
        passing_kernel,
        grid_spec=pltpu.PrefetchScalarGridSpec(
            num_scalar_prefetch=2,
            grid=(heads.shape[0],),
            in_specs=[
                pl.BlockSpec((rows, D), head),
                pl.BlockSpec((rows, D), key),
                pl.BlockSpec((rows, D), value),
                pl.BlockSpec((WIN, D), key),
                pl.BlockSpec((WIN, D), value),
                pl.BlockSpec((SINK, D), sink_key),
                pl.BlockSpec((SINK, D), sink_value),
            ],
            out_specs=pl.BlockSpec((rows, D), head),
            scratch_shapes=[
                pltpu.VMEM((D, SINK + WIN + rows), jnp.bfloat16),
                pltpu.VMEM((SINK + WIN + rows, 2 * D), jnp.bfloat16),
            ],
        ),
        out_shape=jax.ShapeDtypeStruct((rows, width), jnp.bfloat16),
        compiler_params=pltpu.CompilerParams(vmem_limit_bytes=VMEM_LIMIT),
        cost_estimate=pl.CostEstimate(
            flops=4 * width * rows * (SINK + WIN + QB) * 2,
            bytes_accessed=4 * rows * width,
            transcendentals=width // D * rows * (SINK + WIN + QB),
        ),
        name="passing_heads",
    )(heads, used, q, kv, kv, previous, previous, shared, shared)


def retrieval_kernel(
    heads, used, counts, offsets, q, k, v, pk, pv, far_k, far_v, old, out, keys, vals, sem
):
    i = pl.program_id(0)
    rows = q.shape[0]

    @pl.when(new_group(heads, i))
    def _():
        keys[:WIN, :] = pk[...]
        keys[WIN:, :] = k[...]
        vals[:WIN, :D] = pv[...]
        vals[WIN:, :D] = v[...]
        vals[:, D:] = jnp.ones_like(vals[:, D:])

    @pl.when((i == 0) & (used[0] == 0))
    def _():
        copy = pltpu.make_async_copy(old.at[:, pl.ds(0, D)], out, sem)
        copy.start()
        copy.wait()

    @pl.when(i < used[0])
    def _():
        row = lax.broadcasted_iota(jnp.int32, (BLK, NSL * BLK), 0)
        col = lax.broadcasted_iota(jnp.int32, (BLK, NSL * BLK), 1)
        causal = (col <= row) | (col >= BLK)
        lane = lax.broadcasted_iota(jnp.int32, (1, VB * BLK), 1)
        open_cols = lane < counts[i] * BLK
        vert_k = far_k[...]
        vert_v = jnp.concatenate([far_v[...], jnp.ones((VB * BLK, D), jnp.bfloat16)], 1)
        for r in range(0, rows, QB):
            q_rows = q[r : r + QB, :]
            s_vert = jnp.where(open_cols, dot_nt(q_rows, vert_k), -jnp.inf)
            p_verts, slashes = [], []
            for b in range(0, QB, BLK):
                picks = [
                    pl.ds(
                        pl.multiple_of((WIN + r + b) - offsets[i * NSL + t] * BLK, BLK), BLK
                    )
                    for t in range(NSL)
                ]
                near_k = jnp.concatenate([keys[pick, :] for pick in picks], 0)
                near_v = jnp.concatenate([vals[pick, :] for pick in picks], 0)
                s_near = jnp.where(causal, dot_nt(q_rows[b : b + BLK], near_k), -jnp.inf)
                s_far = s_vert[b : b + BLK]
                top = jnp.maximum(
                    jnp.max(s_near, axis=1, keepdims=True), jnp.max(s_far, axis=1, keepdims=True)
                )
                p_near = jnp.exp2((s_near - top) * SCALE).astype(jnp.bfloat16)
                p_verts.append(jnp.exp2((s_far - top) * SCALE).astype(jnp.bfloat16))
                slashes.append(dot(p_near, near_v))
            acc = dot(jnp.concatenate(p_verts, 0), vert_v) + jnp.concatenate(slashes, 0)
            out[r : r + QB, :] = (acc[:, :D] / acc[:, D:]).astype(out.dtype)


def retrieval(heads, used, counts, offsets, q, kv, previous, shared, old):
    rows, width = q.shape
    kv_count = kv.shape[1] // (2 * D)
    slots = heads.shape[0]

    def head(i, heads, *_):
        return (0, heads[i])

    def key(i, heads, *_):
        return (0, heads[i] // SHARE)

    def value(i, heads, *_):
        return (0, kv_count + heads[i] // SHARE)

    def slot(i, heads, used, *_):
        return (jnp.maximum(jnp.minimum(i, used[0] - 1), 0), 0)

    def slot_value(i, heads, used, *_):
        return (slots + jnp.maximum(jnp.minimum(i, used[0] - 1), 0), 0)

    return pl.pallas_call(
        retrieval_kernel,
        grid_spec=pltpu.PrefetchScalarGridSpec(
            num_scalar_prefetch=4,
            grid=(slots,),
            in_specs=[
                pl.BlockSpec((rows, D), head),
                pl.BlockSpec((rows, D), key),
                pl.BlockSpec((rows, D), value),
                pl.BlockSpec((WIN, D), key),
                pl.BlockSpec((WIN, D), value),
                pl.BlockSpec((VB * BLK, D), slot),
                pl.BlockSpec((VB * BLK, D), slot_value),
                pl.BlockSpec(memory_space=pl.ANY),
            ],
            out_specs=pl.BlockSpec((rows, D), head),
            scratch_shapes=[
                pltpu.VMEM((WIN + rows, D), jnp.bfloat16),
                pltpu.VMEM((WIN + rows, 2 * D), jnp.bfloat16),
                pltpu.SemaphoreType.DMA,
            ],
        ),
        out_shape=jax.ShapeDtypeStruct((rows, width), jnp.bfloat16),
        input_output_aliases={11: 0},
        compiler_params=pltpu.CompilerParams(vmem_limit_bytes=VMEM_LIMIT),
        cost_estimate=pl.CostEstimate(
            flops=4 * slots * D * rows * (VB + NSL) * BLK * 2,
            bytes_accessed=4 * rows * slots * D,
            transcendentals=slots * rows * (VB + NSL) * BLK,
        ),
        name="retrieval_heads",
    )(heads, used, counts, offsets, q, kv, kv, previous, previous, shared, shared, old)


def compact(flags, length):
    n = flags.shape[0]
    place = jnp.arange(n, dtype=jnp.int32)
    rank = jnp.sum(jnp.where(place[None, :] < place[:, None], flags[None, :], 0), 1)
    used = jnp.sum(flags)
    wanted = jnp.minimum(jnp.arange(length, dtype=jnp.int32), used - 1)
    hit = (rank[None, :] == wanted[:, None]) & (flags[None, :] == 1)
    return jnp.sum(jnp.where(hit, place[None, :], 0), 1).astype(jnp.int32), used


def exchange(block):
    return lax.all_to_all(block, "head", split_axis=1, concat_axis=0, tiled=True)


def shards(queries, keys, values, prefix_keys, prefix_values, roles, columns, col_count, diagonals):
    seq_size = lax.axis_size("seq")
    head_size = lax.axis_size("head")
    my_seq = lax.axis_index("seq")
    cache_rows, cache_width = prefix_keys.shape
    kv_count = cache_width // D
    heads_here = kv_count * SHARE
    slots = kv_count * MAX_RETRIEVERS

    finders, finder_count = compact(jnp.where(roles == 1, 1, 0), slots)
    passers, passer_count = compact(jnp.where(roles == 1, 0, 1), heads_here)
    cols = columns[finders]
    counts = col_count[finders]
    offsets = diagonals[finders].reshape(-1)
    blocks_dev = cache_rows // BLK
    used_col = (jnp.arange(VB)[None, :] < counts[:, None]) & (
        jnp.arange(slots)[:, None] < finder_count
    )
    own = ((cols // blocks_dev == my_seq) & used_col).astype(jnp.int32).reshape(-1)
    local = (cols % blocks_dev).reshape(-1)
    kv_of = jnp.broadcast_to((finders // SHARE)[:, None], (slots, VB)).reshape(-1)
    own = jnp.concatenate([own, (my_seq == 0).astype(jnp.int32).reshape(1)])
    sink_at = 2 * slots * VB * BLK
    unit = 2 * 16 * seq_size
    shared_rows = -(-(sink_at + 2 * kv_count * SINK) // unit) * unit
    mine = collect(own, local, kv_of, prefix_keys, prefix_values, shared_rows)
    shared = share(mine)

    rows_in = keys.shape[0]
    kv_out = jnp.concatenate(
        [
            keys.reshape(rows_in, head_size, cache_width),
            values.reshape(rows_in, head_size, cache_width),
        ],
        2,
    ).reshape(rows_in, head_size * 2 * cache_width)
    kv = exchange(kv_out)
    q = exchange(queries)
    tail_cache = jnp.concatenate(
        [prefix_keys[cache_rows - WIN :], prefix_values[cache_rows - WIN :]], 1
    )
    outgoing = jnp.where(my_seq == seq_size - 1, tail_cache, kv[kv.shape[0] - WIN :])
    route = [(i, (i + 1) % seq_size) for i in range(seq_size)]
    previous = lax.ppermute(outgoing, "seq", route)

    out = passing(passers, passer_count.reshape(1), q, kv, previous, shared, sink_at // SINK)
    return retrieval(
        finders, finder_count.reshape(1), counts, offsets, q, kv, previous, shared, out
    )


def solution(mesh):
    placed = (
        P(("seq", "head"), None),
        P(("seq", "head"), None),
        P(("seq", "head"), None),
        P("seq", "head"),
        P("seq", "head"),
        P("head"),
        P("head", None),
        P("head"),
        P("head", None),
    )
    return jax.shard_map(
        shards, mesh=mesh, in_specs=placed, out_specs=P("seq", "head"), check_vma=False
    )
```

profile of v0, /device:TPU:5, one launch (start us, length us, event | category | flops | bytes accessed | tf_op | source)
XLA Modules:
  0.0 159.3 jit_solution(10894516068580293626)
XLA Ops:
  0.0 0.0 copy-start
  0.0 1.3 copy_bitcast_fusion.1
  1.3 0.0 copy-start.7
  1.3 1.1 pad_maximum_fusion
  2.4 3.6 %all-to-all-start.1 = ((bf16[256,2,1024]{2,0,1:T(8,128)(2,1)}), bf16[256,2,1024]{2,0,1:T(8,128)(2,1)S(1)}, u32[]{:S(2)}, u32[]{:S(2)}) async-start(bf16[256,2,1024]{2,0,1:T(8,128)(2,1)} %pad_maximum_fusion), calls=%async_computation.1 | async-start | bytes 2097152 | tf_op jit(solution)/shard_map/all_to_all | solution.py:430
  6.0 0.0 copy-done.7
  6.0 0.7 fusion.3
  7.3 0.1 select_reduce_fusion.1
  7.5 0.2 select_reduce_fusion.3.heads
  7.7 4.7 %copy.32 = bf16[32,2,8,4096]{3,2,0,1:T(8,128)(2,1)} copy(bf16[32,2,8,4096]{3,2,1,0:T(8,128)(2,1)} %bitcast.29) | data formatting | bytes 8388608 | tf_op jit(solution)/shard_map/all_to_all | solution.py:430
  12.4 0.0 copy-done
  12.4 0.7 gather_fusion
  13.0 0.6 iota_compare_fusion.2
  13.7 0.1 fusion
  13.8 3.4 %all-to-all-done.1 = bf16[256,2,1024]{2,0,1:T(8,128)(2,1)S(1)} async-done(((bf16[256,2,1024]{2,0,1:T(8,128)(2,1)}), bf16[256,2,1024]{2,0,1:T(8,128)(2,1)S(1)}, u32[]{:S(2)}, u32[]{:S(2)}) %all-to-all-start.1) | async-done | bytes 1048608 | tf_op jit(solution)/shard_map/all_to_all | solution.py:430
  17.2 0.0 copy-start.5
  17.2 0.0 copy-start.6
  17.2 7.8 %all-to-all-start = ((bf16[256,2,4096]{2,0,1:T(8,128)(2,1)}), bf16[256,2,4096]{2,0,1:T(8,128)(2,1)}, u32[]{:S(2)}, u32[]{:S(2)}) async-start(bf16[256,2,4096]{2,0,1:T(8,128)(2,1)} %bitcast.28), calls=%async_computation | async-start | bytes 8388608 | tf_op jit(solution)/shard_map/all_to_all | solution.py:430
  25.0 0.0 copy-start.3
  25.8 0.1 and.64
  25.9 0.1 broadcast_in_dim.77
  26.0 0.1 reshape.95.kv_of
  26.1 0.0 copy-done.5
  26.1 0.1 copy.25
  26.2 0.6 gather_fusion.2
  26.7 0.1 gather.14
  26.8 0.0 copy-done.6
  26.8 0.1 copy.21
  26.9 0.6 gather_fusion.1
  27.5 0.1 reshape.91.offsets
  27.6 0.1 add_convert_fusion.own
  27.7 0.0 copy-done.3
  27.7 0.0 copy-start.4
  27.7 1.6 copy-done.4
  29.3 0.0 slice-start
  29.3 0.0 slice-start.1
  29.3 5.2 %collect_columns.1.mine = bf16[13312,128]{1,0:T(8,128)(2,1)S(1)} custom-call(s32[97]{0:T(128)S(1)} %add_convert_fusion.own, s32[96]{0:T(128)S(1)} %and_select_fusion.1.blk, s32[96]{0:T(128)S(1)} %reshape.95.kv_of, bf16[2048,512]{1,0:T(8,128)(2,1)S(1)} %copy-done.4, bf16[2048,512]{1,0:T(8,128)(2,1)S(1)} %copy-done.3), custom_call_target="tpu_custom_call" | custom-call | tf_op jit(solution)/shard_map/collect_columns/pallas_call | solution.py:94
  34.5 0.0 slice-done
  34.5 0.0 slice-done.1
  34.5 0.4 maximum_select_fusion
  35.0 2.9 %collective-permute-start = (bf16[512,1024]{1,0:T(8,128)(2,1)S(1)}, bf16[512,1024]{1,0:T(8,128)(2,1)S(1)}, u32[]{:S(2)}, u32[]{:S(2)}) collective-permute-start(bf16[512,1024]{1,0:T(8,128)(2,1)S(1)} %maximum_select_fusion), channel_id=1, source_target_pairs={{0,2},{2,4},{4,6},{6,8},{8,10},{10,12},{12,14},{14,16},{16,18},{18... | collective-permute-start | bytes 3145736 | tf_op jit(solution)/shard_map/ppermute | solution.py:476
  37.8 0.2 select_reduce_fusion.heads
  38.0 67.7 %share_columns.1.sk.sv.far_k.far_v = bf16[13312,128]{1,0:T(8,128)(2,1)S(1)} custom-call(bf16[13312,128]{1,0:T(8,128)(2,1)S(1)} %collect_columns.1.mine), custom_call_target="tpu_custom_call" | custom-call | flops 10000000000 | bytes 13631488 | tf_op jit(solution)/shard_map/share_columns/pallas_call | solution.py:198
  105.8 0.0 copy-start.1
  105.8 1.8 %copy-done.1 = bf16[13312,128]{1,0:T(8,128)(2,1)} copy-done((bf16[13312,128]{1,0:T(8,128)(2,1)}, bf16[13312,128]{1,0:T(8,128)(2,1)S(1)}, u32[]{:S(2)}) %copy-start.1) | copy-done | bytes 3407896
  107.5 0.0 collective-permute-done.pk.pv
  107.5 0.0 all-to-all-done
  107.5 0.0 copy-start.2
  107.5 2.0 %copy-done.2 = bf16[13312,128]{1,0:T(8,128)(2,1)S(1)} copy-done((bf16[13312,128]{1,0:T(8,128)(2,1)S(1)}, bf16[13312,128]{1,0:T(8,128)(2,1)}, u32[]{:S(2)}) %copy-start.2) | copy-done | bytes 3407896
  109.5 36.7 %passing_heads.1.old = bf16[512,4096]{1,0:T(8,128)(2,1)} custom-call(s32[32]{0:T(128)S(1)} %select_reduce_fusion.heads, s32[1]{0:T(128)} %bitcast.9.used, bf16[512,4096]{1,0:T(8,128)(2,1)} %bitcast.4.q, bf16[512,1024]{1,0:T(8,128)(2,1)S(1)} %bitcast.24, bf16[512,1024]{1,0:T(8,128)(2,1)S(1)} %bitcast.25, bf16[512,1024]{1,0:T(8,128)(2,1)S(1)} %collective-permute-done.pk.pv, ...), custom_call_target="tpu_custom_call" | custom-call | flops 12884901888 | bytes 8388608 | tf_op jit(solution)/shard_map/passing_heads/pallas_call | solution.py:280
  146.2 13.1 %retrieval_heads.1 = bf16[512,4096]{1,0:T(8,128)(2,1)} custom-call(s32[16]{0:T(128)S(1)} %select_reduce_fusion.3.heads, s32[1]{0:T(128)} %bitcast.used, s32[16]{0:T(128)S(1)} %gather_fusion, s32[64]{0:T(128)S(1)} %reshape.91.offsets, bf16[512,4096]{1,0:T(8,128)(2,1)} %bitcast.4.q, bf16[512,1024]{1,0:T(8,128)(2,1)S(1)} %bitcast.26, ...), custom_call_target="tpu_custom_call", output_to_operand_aliasing={{}: (11, {})} | custom-call | flops 5368709120 | bytes 4194304 | tf_op jit(solution)/shard_map/retrieval_heads/pallas_call | solution.py:385
  (8 shorter events, 0.1 us)
Async XLA Ops:
  0.0 12.4 %copy-start = (s32[32]{0:T(128)S(1)}, s32[32]{0:T(128)}, u32[]{:S(2)}) copy-start(s32[32]{0:T(128)} %param.16) | copy-start | bytes 388
  1.3 4.7 %copy-start.7 = (s32[32]{0:T(128)S(1)}, s32[32]{0:T(128)}, u32[]{:S(2)}) copy-start(s32[32]{0:T(128)} %param.14) | copy-start | bytes 388
  2.4 14.8 %all-to-all-start.1 = ((bf16[256,2,1024]{2,0,1:T(8,128)(2,1)}), bf16[256,2,1024]{2,0,1:T(8,128)(2,1)S(1)}, u32[]{:S(2)}, u32[]{:S(2)}) async-start(bf16[256,2,1024]{2,0,1:T(8,128)(2,1)} %pad_maximum_fusion), calls=%async_computation.1 | async-start | bytes 2097152 | tf_op jit(solution)/shard_map/all_to_all | solution.py:430
  17.2 8.9 %copy-start.5 = (s32[32,6]{0,1:T(8,128)S(1)}, s32[32,6]{0,1:T(8,128)}, u32[]{:S(2)}) copy-start(s32[32,6]{0,1:T(8,128)} %param.15) | copy-start | bytes 2308
  17.2 9.6 %copy-start.6 = (s32[32,4]{0,1:T(4,128)S(1)}, s32[32,4]{0,1:T(4,128)}, u32[]{:S(2)}) copy-start(s32[32,4]{0,1:T(4,128)} %param.17) | copy-start | bytes 1540
  17.2 90.3 %all-to-all-start = ((bf16[256,2,4096]{2,0,1:T(8,128)(2,1)}), bf16[256,2,4096]{2,0,1:T(8,128)(2,1)}, u32[]{:S(2)}, u32[]{:S(2)}) async-start(bf16[256,2,4096]{2,0,1:T(8,128)(2,1)} %bitcast.28), calls=%async_computation | async-start | bytes 8388608 | tf_op jit(solution)/shard_map/all_to_all | solution.py:430
  25.0 2.7 %copy-start.3 = (bf16[2048,512]{1,0:T(8,128)(2,1)S(1)}, bf16[2048,512]{1,0:T(8,128)(2,1)}, u32[]{:S(2)}) copy-start(bf16[2048,512]{1,0:T(8,128)(2,1)} %pv.1) | copy-start | bytes 6291460
  27.7 1.6 %copy-start.4 = (bf16[2048,512]{1,0:T(8,128)(2,1)S(1)}, bf16[2048,512]{1,0:T(8,128)(2,1)}, u32[]{:S(2)}) copy-start(bf16[2048,512]{1,0:T(8,128)(2,1)} %pk.1) | copy-start | bytes 6291460
  29.3 5.2 %slice-start = ((bf16[2048,512]{1,0:T(8,128)(2,1)}), bf16[512,512]{1,0:T(8,128)(2,1)S(1)}, s32[]{:S(2)}) async-start(bf16[2048,512]{1,0:T(8,128)(2,1)} %pv.1), calls=%async_computation.2 | async-start | bytes 1048576 | tf_op jit(solution)/shard_map/slice | solution.py:472
  29.3 5.3 %slice-start.1 = ((bf16[2048,512]{1,0:T(8,128)(2,1)}), bf16[512,512]{1,0:T(8,128)(2,1)S(1)}, s32[]{:S(2)}) async-start(bf16[2048,512]{1,0:T(8,128)(2,1)} %pk.1), calls=%async_computation.3 | async-start | bytes 1048576 | tf_op jit(solution)/shard_map/slice | solution.py:472
  35.0 72.6 %collective-permute-start = (bf16[512,1024]{1,0:T(8,128)(2,1)S(1)}, bf16[512,1024]{1,0:T(8,128)(2,1)S(1)}, u32[]{:S(2)}, u32[]{:S(2)}) collective-permute-start(bf16[512,1024]{1,0:T(8,128)(2,1)S(1)} %maximum_select_fusion), channel_id=1, source_target_pairs={{0,2},{2,4},{4,6},{6,8},{8,10},{10,12},{12,14},{14,16},{16,18},{18... | collective-permute-start | bytes 3145736 | tf_op jit(solution)/shard_map/ppermute | solution.py:476
  105.8 1.8 %copy-start.1 = (bf16[13312,128]{1,0:T(8,128)(2,1)}, bf16[13312,128]{1,0:T(8,128)(2,1)S(1)}, u32[]{:S(2)}) copy-start(bf16[13312,128]{1,0:T(8,128)(2,1)S(1)} %share_columns.1.sk.sv.far_k.far_v) | copy-start | bytes 10223620
  107.5 2.0 %copy-start.2 = (bf16[13312,128]{1,0:T(8,128)(2,1)S(1)}, bf16[13312,128]{1,0:T(8,128)(2,1)}, u32[]{:S(2)}) copy-start(bf16[13312,128]{1,0:T(8,128)(2,1)} %copy-done.1) | copy-start | bytes 10223620
where the time goes:
time: 161 us; the launch traced here: 159 us
  Pallas kernels  123 us (76%)
  starting transfers between devices  14.3 us (9%)
  local copies, waits for them, and re-layouts  13.7 us (9%)
  other arithmetic  3.53 us (2%)
  waiting for transfers between devices  3.45 us (2%)
    pallas_call x1, Pallas kernels, share(): pl.pallas_call(functools.partial(share_kernel, size, orders), out_shape=j...  67.7 us
    pallas_call x1, Pallas kernels, passing(): pl.pallas_call(passing_kernel, grid_spec=pltpu.PrefetchScalarGridSpec(num...  36.7 us
    pallas_call x1, Pallas kernels, retrieval(): pl.pallas_call(retrieval_kernel, grid_spec=pltpu.PrefetchScalarGridSpec(n...  13.1 us
    all_to_all x2, starting transfers between devices, exchange(): lax.all_to_all(block, 'head', split_axis=1, concat_axis=0, tiled=True)  11.4 us
    unnamed x18, local copies, waits for them, and re-layouts  5.5 us
    pallas_call x1, Pallas kernels, collect(): pl.pallas_call(collect_kernel, grid_spec=pltpu.PrefetchScalarGridSpec(num...  5.22 us
    all_to_all x1, local copies, waits for them, and re-layouts, exchange(): lax.all_to_all(block, 'head', split_axis=1, concat_axis=0, tiled=True)  4.7 us
    all_to_all x2, waiting for transfers between devices, exchange(): lax.all_to_all(block, 'head', split_axis=1, concat_axis=0, tiled=True)  3.45 us
  transfers between devices with their start and end apart: 3, of which 1 were waited for; matrix products, arithmetic and copies ran while one was open for 6% of the time, Pallas kernels for 46%

commit v1 on v0

--- a/solution.py
+++ b/solution.py
@@ -96,7 +96,7 @@
         grid_spec=pltpu.PrefetchScalarGridSpec(
             num_scalar_prefetch=3,
             grid=(1,),
-            in_specs=[pl.BlockSpec(memory_space=pl.ANY)] * 2,
+            in_specs=[pl.BlockSpec(memory_space=pltpu.HBM)] * 2,
             out_specs=pl.BlockSpec((rows, D), lambda i, *_: (0, 0)),
             scratch_shapes=[
                 pltpu.SemaphoreType.DMA((2, count)),
@@ -109,8 +109,33 @@
     )(own, blk, kv_of, prefix_keys, prefix_values)
 
 
-def share_kernel(size, orders, mine, out, acc, landed, send_sem, recv_sem):
+def share_kernel(
+    size,
+    heads,
+    orders,
+    mine,
+    queries,
+    keys,
+    values,
+    cache_k,
+    cache_v,
+    out,
+    q_out,
+    kv_out,
+    previous,
+    acc,
+    landed,
+    send_sem,
+    recv_sem,
+    swap_send,
+    swap_recv,
+    tail_send,
+    tail_recv,
+    own_sem,
+):
     me = lax.axis_index("seq")
+    my_head = lax.axis_index("head")
+    right, left = lax.rem(me + 1, size), lax.rem(me + size - 1, size)
     bits = len(orders[0])
     barrier = pltpu.get_barrier_semaphore()
 
@@ -124,7 +149,81 @@
         pl.semaphore_signal(
             barrier, inc=1, device_id={"seq": partner(b)}, device_id_type=pl.DeviceIdType.MESH
         )
-    pl.semaphore_wait(barrier, bits)
+    for d in range(1, heads):
+        pl.semaphore_signal(
+            barrier,
+            inc=1,
+            device_id={"head": lax.rem(my_head + d, heads)},
+            device_id_type=pl.DeviceIdType.MESH,
+        )
+    for neighbour in (left, right):
+        pl.semaphore_signal(
+            barrier, inc=1, device_id={"seq": neighbour}, device_id_type=pl.DeviceIdType.MESH
+        )
+    pl.semaphore_wait(barrier, bits + heads + 1)
+
+    rows_in, cache_width = keys.shape[0], cache_k.shape[1]
+    my_rows = pl.ds(pl.multiple_of(my_head * rows_in, 16), rows_in)
+    swaps = (
+        (keys, kv_out.at[my_rows, pl.ds(0, cache_width)], cache_width),
+        (values, kv_out.at[my_rows, pl.ds(cache_width, cache_width)], cache_width),
+        (queries, q_out.at[my_rows, :], q_out.shape[1]),
+    )
+    swapped = []
+    for n, (source, target, width) in enumerate(swaps):
+        row = []
+        for d in range(heads):
+            to = lax.rem(my_head + d, heads)
+            block = source.at[:, pl.ds(pl.multiple_of(to * width, D), width)]
+            if d == 0:
+                copy = pltpu.make_async_copy(block, target, own_sem.at[n])
+            else:
+                copy = pltpu.make_async_remote_copy(
+                    src_ref=block,
+                    dst_ref=target,
+                    send_sem=swap_send.at[n, d - 1],
+                    recv_sem=swap_recv.at[n, d - 1],
+                    device_id={"head": to},
+                    device_id_type=pl.DeviceIdType.MESH,
+                )
+            copy.start()
+            row.append(copy)
+        swapped.append(row)
+
+    def tails(cached):
+        copies = []
+        for n, cache in enumerate((cache_k, cache_v)):
+            place = pl.ds(n * cache_width, cache_width)
+            if cached:
+                source = cache.at[pl.ds(cache.shape[0] - WIN, WIN), :]
+            else:
+                source = kv_out.at[pl.ds(kv_out.shape[0] - WIN, WIN), place]
+            copies.append(
+                pltpu.make_async_remote_copy(
+                    src_ref=source,
+                    dst_ref=previous.at[:, place],
+                    send_sem=tail_send.at[n],
+                    recv_sem=tail_recv.at[n],
+                    device_id={"seq": right},
+                    device_id_type=pl.DeviceIdType.MESH,
+                )
+            )
+        return copies
+
+    def pass_tails():
+        for row in swapped[:2]:
+            for copy in row:
+                copy.wait()
+
+        @pl.when(me == size - 1)
+        def _():
+            for copy in tails(True):
+                copy.start()
+
+        @pl.when(me != size - 1)
+        def _():
+            for copy in tails(False):
+                copy.start()
 
     streams = len(orders)
     part = mine.shape[0] // streams
@@ -188,23 +287,44 @@
                 halve(w, step)
             elif step < 2 * bits:
                 double(w, step)
-
-
-def share(mine):
-    size = lax.axis_size("seq")
+        if step == 1:
+            pass_tails()
+    for copy in tails(False):
+        copy.wait()
+    for copy in swapped[2]:
+        copy.wait()
+
+
+def share(mine, queries, keys, values, prefix_keys, prefix_values):
+    size, heads = lax.axis_size("seq"), lax.axis_size("head")
     bits = size.bit_length() - 1
     orders = [list(range(bits)), [0, *range(2, bits), 1]]
     rows = mine.shape[0]
+    kind = mine.dtype
+    span = keys.shape[0] * heads
+    cache_width = prefix_keys.shape[1]
+    anywhere = pl.BlockSpec(memory_space=pltpu.HBM)
+    local = pl.BlockSpec(memory_space=pltpu.VMEM)
     return pl.pallas_call(
-        functools.partial(share_kernel, size, orders),
-        out_shape=jax.ShapeDtypeStruct(mine.shape, mine.dtype),
-        in_specs=[pl.BlockSpec(memory_space=pltpu.VMEM)],
-        out_specs=pl.BlockSpec(memory_space=pltpu.VMEM),
+        functools.partial(share_kernel, size, heads, orders),
+        out_shape=(
+            jax.ShapeDtypeStruct(mine.shape, kind),
+            jax.ShapeDtypeStruct((span, queries.shape[1] // heads), kind),
+            jax.ShapeDtypeStruct((span, 2 * cache_width), kind),
+            jax.ShapeDtypeStruct((WIN, 2 * cache_width), kind),
+        ),
+        in_specs=[local] + [anywhere] * 5,
+        out_specs=(local, anywhere, anywhere, anywhere),
         scratch_shapes=[
-            pltpu.VMEM((rows, D), mine.dtype),
-            pltpu.VMEM((rows, D), mine.dtype),
+            pltpu.VMEM((rows, D), kind),
+            pltpu.VMEM((rows, D), kind),
             pltpu.SemaphoreType.DMA((len(orders), 2 * bits)),
             pltpu.SemaphoreType.DMA((len(orders), 2 * bits)),
+            pltpu.SemaphoreType.DMA((3, heads - 1)),
+            pltpu.SemaphoreType.DMA((3, heads - 1)),
+            pltpu.SemaphoreType.DMA((2,)),
+            pltpu.SemaphoreType.DMA((2,)),
+            pltpu.SemaphoreType.DMA((3,)),
         ],
         compiler_params=pltpu.CompilerParams(
             collective_id=0, has_side_effects=True, vmem_limit_bytes=VMEM_LIMIT
@@ -213,7 +333,7 @@
             flops=10**10, bytes_accessed=8 * rows * D, transcendentals=0
         ),
         name="share_columns",
-    )(mine)
+    )(mine, queries, keys, values, prefix_keys, prefix_values)
 
 
 def new_group(heads, i):
@@ -426,13 +546,8 @@
     return jnp.sum(jnp.where(hit, place[None, :], 0), 1).astype(jnp.int32), used
 
 
-def exchange(block):
-    return lax.all_to_all(block, "head", split_axis=1, concat_axis=0, tiled=True)
-
-
 def shards(queries, keys, values, prefix_keys, prefix_values, roles, columns, col_count, diagonals):
     seq_size = lax.axis_size("seq")
-    head_size = lax.axis_size("head")
     my_seq = lax.axis_index("seq")
     cache_rows, cache_width = prefix_keys.shape
     kv_count = cache_width // D
@@ -456,25 +571,9 @@
     unit = 2 * 16 * seq_size
     shared_rows = -(-(sink_at + 2 * kv_count * SINK) // unit) * unit
     mine = collect(own, local, kv_of, prefix_keys, prefix_values, shared_rows)
-    shared = share(mine)
-
-    rows_in = keys.shape[0]
-    kv_out = jnp.concatenate(
-        [
-            keys.reshape(rows_in, head_size, cache_width),
-            values.reshape(rows_in, head_size, cache_width),
-        ],
-        2,
-    ).reshape(rows_in, head_size * 2 * cache_width)
-    kv = exchange(kv_out)
-    q = exchange(queries)
-    tail_cache = jnp.concatenate(
-        [prefix_keys[cache_rows - WIN :], prefix_values[cache_rows - WIN :]], 1
+    shared, q, kv, previous = share(
+        mine, queries, keys, values, prefix_keys, prefix_values
     )
-    outgoing = jnp.where(my_seq == seq_size - 1, tail_cache, kv[kv.shape[0] - WIN :])
-    route = [(i, (i + 1) % seq_size) for i in range(seq_size)]
-    previous = lax.ppermute(outgoing, "seq", route)
-
     out = passing(passers, passer_count.reshape(1), q, kv, previous, shared, sink_at // SINK)
     return retrieval(
         finders, finder_count.reshape(1), counts, offsets, q, kv, previous, shared, out

time: 161 us -> 143 us (0.89)
  starting transfers between devices: 14.3 us -> 0 us
  Pallas kernels: 123 us -> 128 us
  local copies, waits for them, and re-layouts: 13.7 us -> 9.13 us
  waiting for transfers between devices: 3.45 us -> 0 us
    all_to_all x2 -> x0, starting transfers between devices: 11.4 us -> none  [exchange(): lax.all_to_all(block, 'head', split_axis=1, concat_axis=0, tiled=True)]
    pallas_call x1, Pallas kernels: 13.1 us -> 20.2 us  [retrieval(): pl.pallas_call(retrieval_kernel, grid_spec=pltpu.PrefetchScalarGridSpec(n...]
    pallas_call x1, Pallas kernels: 36.7 us -> 30.2 us  [passing(): pl.pallas_call(passing_kernel, grid_spec=pltpu.PrefetchScalarGridSpec(num...]
    pallas_call x1, Pallas kernels: 67.7 us -> 72.5 us  [share(): pl.pallas_call(functools.partial(share_kernel, size, heads, orders), out_...]
    all_to_all x1 -> x0, local copies, waits for them, and re-layouts: 4.7 us -> none  [exchange(): lax.all_to_all(block, 'head', split_axis=1, concat_axis=0, tiled=True)]
    all_to_all x2 -> x0, waiting for transfers between devices: 3.45 us -> none  [exchange(): lax.all_to_all(block, 'head', split_axis=1, concat_axis=0, tiled=True)]
    ppermute x1 -> x0, starting transfers between devices: 2.88 us -> none  [shards(): previous = lax.ppermute(outgoing, 'seq', route)]
  transfers between devices with their start and end apart: 3 -> 0, of which waited for: 1 -> 0; matrix products, arithmetic and copies ran while one was open for 6% -> 0% of each run, Pallas kernels for 46% -> 0%
where the time goes in v1:
time: 143 us; the launch traced here: 142 us
  Pallas kernels  128 us (90%)
  local copies, waits for them, and re-layouts  9.13 us (6%)
  other arithmetic  3.3 us (2%)
    pallas_call x1, Pallas kernels, share(): pl.pallas_call(functools.partial(share_kernel, size, heads, orders), out_...  72.5 us
    pallas_call x1, Pallas kernels, passing(): pl.pallas_call(passing_kernel, grid_spec=pltpu.PrefetchScalarGridSpec(num...  30.2 us
    pallas_call x1, Pallas kernels, retrieval(): pl.pallas_call(retrieval_kernel, grid_spec=pltpu.PrefetchScalarGridSpec(n...  20.2 us
    unnamed x18, local copies, waits for them, and re-layouts  6.91 us
    pallas_call x1, Pallas kernels, collect(): pl.pallas_call(collect_kernel, grid_spec=pltpu.PrefetchScalarGridSpec(num...  5.22 us

profile of v1, /device:TPU:5, one launch (start us, length us, event | category | flops | bytes accessed | tf_op | source)
XLA Modules:
  0.0 142.0 jit_solution(11743157491283841864)
XLA Ops:
  0.0 0.0 copy-start
  0.0 0.7 broadcast_compare_fusion.1
  0.7 1.3 fusion.3
  3.2 0.0 copy-start.6
  3.3 0.1 select_reduce_fusion.1
  3.4 0.2 select_reduce_fusion.3.heads
  3.6 0.2 select_reduce_fusion.heads
  3.8 0.6 iota_compare_fusion.2
  4.4 0.0 copy-done
  4.4 0.7 gather_fusion
  5.1 0.1 fusion
  5.2 0.1 and.64
  5.3 0.1 broadcast_in_dim.77
  5.3 0.1 reshape.79.kv_of
  5.4 0.8 copy.16
  6.2 0.6 gather_fusion.2
  6.8 0.1 gather.14
  6.9 0.1 add_convert_fusion.own
  7.0 0.8 copy.15
  7.7 0.6 gather_fusion.1
  8.3 0.1 reshape.77.offsets
  8.4 0.0 copy-start.2
  8.4 1.6 %copy-done.2 = bf16[2048,512]{1,0:T(8,128)(2,1)S(1)} copy-done((bf16[2048,512]{1,0:T(8,128)(2,1)S(1)}, bf16[2048,512]{1,0:T(8,128)(2,1)}, u32[]{:S(2)}) %copy-start.2) | copy-done | bytes 2097176
  10.0 0.0 copy-start.4
  10.0 1.6 %copy-done.4 = bf16[2048,512]{1,0:T(8,128)(2,1)S(1)} copy-done((bf16[2048,512]{1,0:T(8,128)(2,1)S(1)}, bf16[2048,512]{1,0:T(8,128)(2,1)}, u32[]{:S(2)}) %copy-start.4) | copy-done | bytes 2097176
  11.6 0.0 copy-start.3
  11.6 0.0 copy-start.5
  11.6 0.0 copy-start.7
  11.6 5.2 %collect_columns.1.mine = bf16[13312,128]{1,0:T(8,128)(2,1)S(1)} custom-call(s32[97]{0:T(128)S(1)} %add_convert_fusion.own, s32[96]{0:T(128)S(1)} %and_select_fusion.1.blk, s32[96]{0:T(128)S(1)} %reshape.79.kv_of, bf16[2048,512]{1,0:T(8,128)(2,1)S(1)} %copy-done.2, bf16[2048,512]{1,0:T(8,128)(2,1)S(1)} %copy-done.4), custom_call_target="tpu_custom_call" | custom-call | tf_op jit(solution)/shard_map/collect_columns/pallas_call | solution.py:94
  16.8 0.0 copy-done.6
  16.8 0.0 copy-done.3
  16.8 0.0 copy-done.5
  16.8 0.0 copy-done.7
  16.8 72.5 %share_columns.1 = (bf16[13312,128]{1,0:T(8,128)(2,1)S(1)}, bf16[512,4096]{1,0:T(8,128)(2,1)}, bf16[512,1024]{1,0:T(8,128)(2,1)S(1)}, bf16[512,1024]{1,0:T(8,128)(2,1)S(1)}) custom-call(bf16[13312,128]{1,0:T(8,128)(2,1)S(1)} %collect_columns.1.mine, bf16[256,8192]{1,0:T(8,128)(2,1)} %queries.1, bf16[256,1024]{1,0:T(8,128)(2,1)S(1)} %copy-done.6, ...), custom_call_target="tpu_custom_call" | custom-call | flops 10000000000 | bytes 13631488 | tf_op jit(solution)/shard_map/share_columns/pallas_call | solution.py:308
  89.4 0.0 copy-start.1
  89.4 2.2 %copy-done.1 = bf16[512,4096]{1,0:T(8,128)(2,1)S(1)} copy-done((bf16[512,4096]{1,0:T(8,128)(2,1)S(1)}, bf16[512,4096]{1,0:T(8,128)(2,1)}, u32[]{:S(2)}) %copy-start.1) | copy-done | bytes 4194328
  91.6 30.2 %passing_heads.1.old = bf16[512,4096]{1,0:T(8,128)(2,1)} custom-call(s32[32]{0:T(128)S(1)} %select_reduce_fusion.heads, s32[1]{0:T(128)} %bitcast.4.used, bf16[512,4096]{1,0:T(8,128)(2,1)S(1)} %copy-done.1, bf16[512,1024]{1,0:T(8,128)(2,1)S(1)} %get-tuple-element.10.k.v, bf16[512,1024]{1,0:T(8,128)(2,1)S(1)} %get-tuple-element.10.k.v, ...), custom_call_target="tpu_custom_call" | custom-call | flops 12884901888 | bytes 8388608 | tf_op jit(solution)/shard_map/passing_heads/pallas_call | solution.py:400
  121.8 20.2 %retrieval_heads.1 = bf16[512,4096]{1,0:T(8,128)(2,1)} custom-call(s32[16]{0:T(128)S(1)} %select_reduce_fusion.3.heads, s32[1]{0:T(128)} %bitcast.used, s32[16]{0:T(128)S(1)} %gather_fusion, s32[64]{0:T(128)S(1)} %reshape.77.offsets, bf16[512,4096]{1,0:T(8,128)(2,1)S(1)} %copy-done.1, ...), custom_call_target="tpu_custom_call", output_to_operand_aliasing={{}: (11, {})} | custom-call | flops 5368709120 | bytes 4194304 | tf_op jit(solution)/shard_map/retrieval_heads/pallas_call | solution.py:505
  (7 shorter events, 0.1 us)
Async XLA Ops:
  0.0 4.4 %copy-start = (s32[32]{0:T(128)S(1)}, s32[32]{0:T(128)}, u32[]{:S(2)}) copy-start(s32[32]{0:T(128)} %param.16) | copy-start | bytes 388
  3.2 13.6 %copy-start.6 = (bf16[256,1024]{1,0:T(8,128)(2,1)S(1)}, bf16[256,1024]{1,0:T(8,128)(2,1)}, u32[]{:S(2)}) copy-start(bf16[256,1024]{1,0:T(8,128)(2,1)} %keys.1) | copy-start | bytes 1572868
  8.4 1.6 %copy-start.2 = (bf16[2048,512]{1,0:T(8,128)(2,1)S(1)}, bf16[2048,512]{1,0:T(8,128)(2,1)}, u32[]{:S(2)}) copy-start(bf16[2048,512]{1,0:T(8,128)(2,1)} %cache_k.1) | copy-start | bytes 6291460
  10.0 1.6 %copy-start.4 = (bf16[2048,512]{1,0:T(8,128)(2,1)S(1)}, bf16[2048,512]{1,0:T(8,128)(2,1)}, u32[]{:S(2)}) copy-start(bf16[2048,512]{1,0:T(8,128)(2,1)} %cache_v.1) | copy-start | bytes 6291460
  11.6 5.2 %copy-start.3 = (bf16[2048,512]{1,0:T(8,128)(2,1)S(1)}, bf16[2048,512]{1,0:T(8,128)(2,1)}, u32[]{:S(2)}) copy-start(bf16[2048,512]{1,0:T(8,128)(2,1)} %cache_k.1) | copy-start | bytes 6291460
  11.6 5.3 %copy-start.5 = (bf16[2048,512]{1,0:T(8,128)(2,1)S(1)}, bf16[2048,512]{1,0:T(8,128)(2,1)}, u32[]{:S(2)}) copy-start(bf16[2048,512]{1,0:T(8,128)(2,1)} %cache_v.1) | copy-start | bytes 6291460
  11.6 5.3 %copy-start.7 = (bf16[256,1024]{1,0:T(8,128)(2,1)S(1)}, bf16[256,1024]{1,0:T(8,128)(2,1)}, u32[]{:S(2)}) copy-start(bf16[256,1024]{1,0:T(8,128)(2,1)} %values.1) | copy-start | bytes 1572868
  89.4 2.2 %copy-start.1 = (bf16[512,4096]{1,0:T(8,128)(2,1)S(1)}, bf16[512,4096]{1,0:T(8,128)(2,1)}, u32[]{:S(2)}) copy-start(bf16[512,4096]{1,0:T(8,128)(2,1)} %get-tuple-element.9.q) | copy-start | bytes 12582916

commit v2 on v1

v2 whole, which is shorter than its diff:
```python
import functools
import math

import jax
import jax.numpy as jnp
from jax import lax
from jax.experimental import pallas as pl
from jax.experimental.pallas import tpu as pltpu
from jax.sharding import PartitionSpec as P

QUERY_HEADS = 64
KEY_VALUE_HEADS = 8
SHARE = QUERY_HEADS // KEY_VALUE_HEADS
D = 128
SINK = 128
WIN = 512
BLK = 64
VB = 6
NSL = 4
MAX_RETRIEVERS = 4
QB = 128
SCALE = math.log2(math.e) / math.sqrt(D)
VMEM_LIMIT = 40 * 1024 * 1024


def dot_nt(a, b):
    return lax.dot_general(a, b, (((1,), (1,)), ((), ())), preferred_element_type=jnp.float32)


def dot(a, b):
    return jnp.dot(a, b, preferred_element_type=jnp.float32)


def collect_kernel(seq, roles, columns, col_count, pk, pv, out, sem, sink_sem):
    blocks_dev = pk.shape[0] // BLK
    kv_count = pk.shape[1] // D
    slots = kv_count * MAX_RETRIEVERS
    out[...] = jnp.zeros_like(out)

    def copies(head, slot, c, col):
        local = col - seq[0] * blocks_dev
        rows = pl.ds(pl.multiple_of(local * BLK, BLK), BLK)
        cols = pl.ds(pl.multiple_of((head // SHARE) * D, D), D)
        t = slot * VB + c
        first = pl.ds(pl.multiple_of(t * BLK, BLK), BLK)
        second = pl.ds(pl.multiple_of((slots * VB + t) * BLK, BLK), BLK)
        return (
            pltpu.make_async_copy(pk.at[rows, cols], out.at[first, :], sem.at[0, t]),
            pltpu.make_async_copy(pv.at[rows, cols], out.at[second, :], sem.at[1, t]),
        )

    def sinks():
        base = 2 * slots * VB * BLK
        return [
            pltpu.make_async_copy(
                ref.at[pl.ds(0, SINK), pl.ds(g * D, D)],
                out.at[pl.ds(base + (part * kv_count + g) * SINK, SINK), :],
                sink_sem.at[part, g],
            )
            for part, ref in enumerate((pk, pv))
            for g in range(kv_count)
        ]

    def each(act):
        def visit(head, rank):
            rank = jnp.where(lax.rem(head, SHARE) == 0, 0, rank)
            chosen = roles[head] == 1

            @pl.when(chosen)
            def _():
                slot = (head // SHARE) * MAX_RETRIEVERS + rank
                for c in range(VB):
                    col = columns[head, c]

                    @pl.when((c < col_count[head]) & (col // blocks_dev == seq[0]))
                    def _():
                        for copy in copies(head, slot, c, col):
                            act(copy)

            return rank + chosen.astype(jnp.int32)

        lax.fori_loop(0, kv_count * SHARE, visit, 0)

        @pl.when(seq[0] == 0)
        def _():
            for copy in sinks():
                act(copy)

    each(lambda copy: copy.start())
    each(lambda copy: copy.wait())


def collect(seq, roles, columns, col_count, prefix_keys, prefix_values, rows):
    kv_count = prefix_keys.shape[1] // D
    return pl.pallas_call(
        collect_kernel,
        grid_spec=pltpu.PrefetchScalarGridSpec(
            num_scalar_prefetch=4,
            grid=(1,),
            in_specs=[pl.BlockSpec(memory_space=pltpu.HBM)] * 2,
            out_specs=pl.BlockSpec((rows, D), lambda i, *_: (0, 0)),
            scratch_shapes=[
                pltpu.SemaphoreType.DMA((2, kv_count * MAX_RETRIEVERS * VB)),
                pltpu.SemaphoreType.DMA((2, kv_count)),
            ],
        ),
        out_shape=jax.ShapeDtypeStruct((rows, D), jnp.bfloat16),
        compiler_params=pltpu.CompilerParams(vmem_limit_bytes=VMEM_LIMIT),
        name="collect_columns",
    )(seq, roles, columns, col_count, prefix_keys, prefix_values)


def share_kernel(
    size,
    heads,
    orders,
    mine,
    queries,
    keys,
    values,
    cache_k,
    cache_v,
    out,
    q_out,
    kv_out,
    previous,
    acc,
    landed,
    send_sem,
    recv_sem,
    swap_send,
    swap_recv,
    tail_send,
    tail_recv,
    own_sem,
):
    me = lax.axis_index("seq")
    my_head = lax.axis_index("head")
    right, left = lax.rem(me + 1, size), lax.rem(me + size - 1, size)
    bits = len(orders[0])
    barrier = pltpu.get_barrier_semaphore()

    def bit_of(b):
        return lax.rem(me // (1 << b), 2)

    def partner(b):
        return me + (1 - 2 * bit_of(b)) * (1 << b)

    for b in range(bits):
        pl.semaphore_signal(
            barrier, inc=1, device_id={"seq": partner(b)}, device_id_type=pl.DeviceIdType.MESH
        )
    for d in range(1, heads):
        pl.semaphore_signal(
            barrier,
            inc=1,
            device_id={"head": lax.rem(my_head + d, heads)},
            device_id_type=pl.DeviceIdType.MESH,
        )
    for neighbour in (left, right):
        pl.semaphore_signal(
            barrier, inc=1, device_id={"seq": neighbour}, device_id_type=pl.DeviceIdType.MESH
        )
    pl.semaphore_wait(barrier, bits + heads + 1)

    rows_in, cache_width = keys.shape[0], cache_k.shape[1]
    my_rows = pl.ds(pl.multiple_of(my_head * rows_in, 16), rows_in)
    swaps = (
        (keys, kv_out.at[my_rows, pl.ds(0, cache_width)], cache_width),
        (values, kv_out.at[my_rows, pl.ds(cache_width, cache_width)], cache_width),
        (queries, q_out.at[my_rows, :], q_out.shape[1]),
    )
    swapped = []
    for n, (source, target, width) in enumerate(swaps):
        row = []
        for d in range(heads):
            to = lax.rem(my_head + d, heads)
            block = source.at[:, pl.ds(pl.multiple_of(to * width, D), width)]
            if d == 0:
                copy = pltpu.make_async_copy(block, target, own_sem.at[n])
            else:
                copy = pltpu.make_async_remote_copy(
                    src_ref=block,
                    dst_ref=target,
                    send_sem=swap_send.at[n, d - 1],
                    recv_sem=swap_recv.at[n, d - 1],
                    device_id={"head": to},
                    device_id_type=pl.DeviceIdType.MESH,
                )
            copy.start()
            row.append(copy)
        swapped.append(row)

    def tails(cached):
        copies = []
        for n, cache in enumerate((cache_k, cache_v)):
            place = pl.ds(n * cache_width, cache_width)
            if cached:
                source = cache.at[pl.ds(cache.shape[0] - WIN, WIN), :]
            else:
                source = kv_out.at[pl.ds(kv_out.shape[0] - WIN, WIN), place]
            copies.append(
                pltpu.make_async_remote_copy(
                    src_ref=source,
                    dst_ref=previous.at[:, place],
                    send_sem=tail_send.at[n],
                    recv_sem=tail_recv.at[n],
                    device_id={"seq": right},
                    device_id_type=pl.DeviceIdType.MESH,
                )
            )
        return copies

    def pass_tails():
        for row in swapped[:2]:
            for copy in row:
                copy.wait()

        @pl.when(me == size - 1)
        def _():
            for copy in tails(True):
                copy.start()

        @pl.when(me != size - 1)
        def _():
            for copy in tails(False):
                copy.start()

    streams = len(orders)
    part = mine.shape[0] // streams
    low = [part * w for w in range(streams)]
    length = [part] * streams
    started = {}

    def at(start, n):
        return pl.ds(pl.multiple_of(start, 16), n)

    def move(src, dst, w, step, b):
        copy = pltpu.make_async_remote_copy(
            src_ref=src,
            dst_ref=dst,
            send_sem=send_sem.at[w, step],
            recv_sem=recv_sem.at[w, step],
            device_id={"seq": partner(b)},
            device_id_type=pl.DeviceIdType.MESH,
        )
        copy.start()
        started[w, step] = copy

    def halve(w, step):
        b = orders[w][step]
        half = length[w] // 2
        source = mine if step == 0 else acc
        other = low[w] + (1 - bit_of(b)) * half
        place = part * w + part - length[w]
        move(source.at[at(other, half), :], landed.at[pl.ds(place, half), :], w, step, b)

    def add(w, step):
        b = orders[w][step]
        half = length[w] // 2
        source = mine if step == 0 else acc
        place = part * w + part - length[w]
        keep = at(low[w] + bit_of(b) * half, half)
        started[w, step].wait()
        into = out if step == bits - 1 else acc
        into[keep, :] = source[keep, :] + landed[pl.ds(place, half), :]
        low[w] = low[w] + bit_of(b) * half
        length[w] = half

    def double(w, step):
        b = orders[w][2 * bits - 1 - step]
        whole = out.at[at(low[w], length[w]), :]
        move(whole, whole, w, step, b)

    def join(w, step):
        b = orders[w][2 * bits - 1 - step]
        started[w, step].wait()
        low[w] = low[w] - bit_of(b) * length[w]
        length[w] = 2 * length[w]

    for step in range(2 * bits + 1):
        for w in range(streams):
            if 0 < step <= bits:
                add(w, step - 1)
            elif step > bits:
                join(w, step - 1)
            if step < bits:
                halve(w, step)
            elif step < 2 * bits:
                double(w, step)
        if step == 1:
            pass_tails()
    for copy in tails(False):
        copy.wait()
    for copy in swapped[2]:
        copy.wait()


def share(mine, queries, keys, values, prefix_keys, prefix_values):
    size, heads = lax.axis_size("seq"), lax.axis_size("head")
    bits = size.bit_length() - 1
    orders = [list(range(bits)), [0, *range(2, bits), 1]]
    rows = mine.shape[0]
    kind = mine.dtype
    span = keys.shape[0] * heads
    cache_width = prefix_keys.shape[1]
    anywhere = pl.BlockSpec(memory_space=pltpu.HBM)
    local = pl.BlockSpec(memory_space=pltpu.VMEM)
    return pl.pallas_call(
        functools.partial(share_kernel, size, heads, orders),
        out_shape=(
            jax.ShapeDtypeStruct(mine.shape, kind),
            jax.ShapeDtypeStruct((span, queries.shape[1] // heads), kind),
            jax.ShapeDtypeStruct((span, 2 * cache_width), kind),
            jax.ShapeDtypeStruct((WIN, 2 * cache_width), kind),
        ),
        in_specs=[local] + [anywhere] * 5,
        out_specs=(local, anywhere, anywhere, anywhere),
        scratch_shapes=[
            pltpu.VMEM((rows, D), kind),
            pltpu.VMEM((rows, D), kind),
            pltpu.SemaphoreType.DMA((len(orders), 2 * bits)),
            pltpu.SemaphoreType.DMA((len(orders), 2 * bits)),
            pltpu.SemaphoreType.DMA((3, heads - 1)),
            pltpu.SemaphoreType.DMA((3, heads - 1)),
            pltpu.SemaphoreType.DMA((2,)),
            pltpu.SemaphoreType.DMA((2,)),
            pltpu.SemaphoreType.DMA((3,)),
        ],
        compiler_params=pltpu.CompilerParams(
            collective_id=0, has_side_effects=True, vmem_limit_bytes=VMEM_LIMIT
        ),
        cost_estimate=pl.CostEstimate(
            flops=10**10, bytes_accessed=8 * rows * D, transcendentals=0
        ),
        name="share_columns",
    )(mine, queries, keys, values, prefix_keys, prefix_values)


def attend_kernel(
    roles,
    col_count,
    diagonals,
    q,
    k,
    v,
    pk,
    pv,
    sk,
    sv,
    far_k,
    far_v,
    out,
    keys_t,
    keys,
    vals,
    passers,
):
    group = pl.program_id(0)
    rows = q.shape[0]

    keys_t[:, :SINK] = sk[...].T
    keys_t[:, SINK : SINK + WIN] = pk[...].T
    keys_t[:, SINK + WIN :] = k[...].T
    keys[:WIN, :] = pk[...]
    keys[WIN:, :] = k[...]
    vals[:SINK, :D] = sv[...]
    vals[SINK : SINK + WIN, :D] = pv[...]
    vals[SINK + WIN :, :D] = v[...]
    vals[:, D:] = jnp.ones_like(vals[:, D:])

    def note(i, used):
        passes = roles[group * SHARE + i] != 1

        @pl.when(passes)
        def _():
            passers[used] = i
            passers[used + 1] = i

        return used + passes.astype(jnp.int32)

    used = lax.fori_loop(0, SHARE, note, 0)

    def lanes(i):
        return pl.ds(pl.multiple_of(i * D, D), D)

    def pass_pair(t, carry):
        pair = [lanes(passers[2 * t]), lanes(passers[2 * t + 1])]
        row = lax.rem(lax.broadcasted_iota(jnp.int32, (2 * QB, QB), 0), QB)
        col = lax.broadcasted_iota(jnp.int32, (2 * QB, QB), 1)
        for r in range(0, rows, QB):
            low, high = SINK + r, SINK + r + WIN + QB
            q_rows = jnp.concatenate([q[r : r + QB, place] for place in pair], 0)
            window = jnp.concatenate([keys_t[:, :SINK], keys_t[:, low:high]], 1)
            s = dot(q_rows, window)
            s = jnp.concatenate(
                [
                    s[:, :SINK],
                    jnp.where(col > row, s[:, SINK : SINK + QB], -jnp.inf),
                    s[:, SINK + QB : SINK + WIN],
                    jnp.where(col <= row, s[:, SINK + WIN :], -jnp.inf),
                ],
                1,
            )
            top = jnp.max(s, axis=1, keepdims=True)
            p = jnp.exp2((s - top) * SCALE).astype(jnp.bfloat16)
            acc = dot(p, jnp.concatenate([vals[:SINK, :], vals[low:high, :]], 0))
            done = (acc[:, :D] / acc[:, D:]).astype(out.dtype)
            for n, place in enumerate(pair):
                out[r : r + QB, place] = done[n * QB : (n + 1) * QB]
        return carry

    lax.fori_loop(0, (used + 1) // 2, pass_pair, 0)

    def retrieve(i, slot):
        head = group * SHARE + i
        chosen = roles[head] == 1

        @pl.when(chosen)
        def _():
            row = lax.broadcasted_iota(jnp.int32, (BLK, NSL * BLK), 0)
            col = lax.broadcasted_iota(jnp.int32, (BLK, NSL * BLK), 1)
            causal = (col <= row) | (col >= BLK)
            lane = lax.broadcasted_iota(jnp.int32, (1, VB * BLK), 1)
            open_cols = lane < col_count[head] * BLK
            place = pl.ds(pl.multiple_of(slot * (VB * BLK), VB * BLK), VB * BLK)
            vert_v = jnp.concatenate(
                [far_v[place, :], jnp.ones((VB * BLK, D), jnp.bfloat16)], 1
            )
            q_head = q[:, lanes(i)]
            s_vert = jnp.where(open_cols, dot_nt(q_head, far_k[place, :]), -jnp.inf)
            p_verts, slashes = [], []
            for r in range(0, rows, BLK):
                starts = [
                    pl.multiple_of(WIN + r - diagonals[head, t] * BLK, BLK) for t in range(NSL)
                ]
                near_k = jnp.concatenate([keys[pl.ds(at, BLK), :] for at in starts], 0)
                near_v = jnp.concatenate([vals[pl.ds(SINK + at, BLK), :] for at in starts], 0)
                s_near = jnp.where(causal, dot_nt(q_head[r : r + BLK], near_k), -jnp.inf)
                s_far = s_vert[r : r + BLK]
                top = jnp.maximum(
                    jnp.max(s_near, axis=1, keepdims=True), jnp.max(s_far, axis=1, keepdims=True)
                )
                p_near = jnp.exp2((s_near - top) * SCALE).astype(jnp.bfloat16)
                p_verts.append(jnp.exp2((s_far - top) * SCALE).astype(jnp.bfloat16))
                slashes.append(dot(p_near, near_v))
            acc = dot(jnp.concatenate(p_verts, 0), vert_v) + jnp.concatenate(slashes, 0)
            out[:, lanes(i)] = (acc[:, :D] / acc[:, D:]).astype(out.dtype)

        return slot + chosen.astype(jnp.int32)

    lax.fori_loop(0, SHARE, retrieve, 0)


def attend(roles, col_count, diagonals, q, kv, previous, shared):
    rows, width = q.shape
    kv_count = kv.shape[1] // (2 * D)
    far_rows = MAX_RETRIEVERS * VB * BLK
    sink_block = 2 * kv_count * far_rows // SINK

    def whole(g, *_):
        return (0, g)

    def value(g, *_):
        return (0, kv_count + g)

    return pl.pallas_call(
        attend_kernel,
        grid_spec=pltpu.PrefetchScalarGridSpec(
            num_scalar_prefetch=3,
            grid=(kv_count,),
            in_specs=[
                pl.BlockSpec((rows, SHARE * D), whole),
                pl.BlockSpec((rows, D), whole),
                pl.BlockSpec((rows, D), value),
                pl.BlockSpec((WIN, D), whole),
                pl.BlockSpec((WIN, D), value),
                pl.BlockSpec((SINK, D), lambda g, *_: (sink_block + g, 0)),
                pl.BlockSpec((SINK, D), lambda g, *_: (sink_block + kv_count + g, 0)),
                pl.BlockSpec((far_rows, D), lambda g, *_: (g, 0)),
                pl.BlockSpec((far_rows, D), lambda g, *_: (kv_count + g, 0)),
            ],
            out_specs=pl.BlockSpec((rows, SHARE * D), whole),
            scratch_shapes=[
                pltpu.VMEM((D, SINK + WIN + rows), jnp.bfloat16),
                pltpu.VMEM((WIN + rows, D), jnp.bfloat16),
                pltpu.VMEM((SINK + WIN + rows, 2 * D), jnp.bfloat16),
                pltpu.SMEM((2 * SHARE,), jnp.int32),
            ],
        ),
        out_shape=jax.ShapeDtypeStruct((rows, width), jnp.bfloat16),
        compiler_params=pltpu.CompilerParams(vmem_limit_bytes=VMEM_LIMIT),
        cost_estimate=pl.CostEstimate(
            flops=8 * width * rows * (SINK + WIN + QB),
            bytes_accessed=4 * rows * width,
            transcendentals=width // D * rows * (SINK + WIN + QB),
        ),
        name="attend",
    )(roles, col_count, diagonals, q, kv, kv, previous, previous, shared, shared, shared, shared)


def shards(queries, keys, values, prefix_keys, prefix_values, roles, columns, col_count, diagonals):
    seq_size = lax.axis_size("seq")
    seq = lax.axis_index("seq").astype(jnp.int32).reshape(1)
    kv_count = prefix_keys.shape[1] // D
    needed = 2 * kv_count * (MAX_RETRIEVERS * VB * BLK + SINK)
    unit = 2 * 16 * seq_size
    rows = -(-needed // unit) * unit
    mine = collect(seq, roles, columns, col_count, prefix_keys, prefix_values, rows)
    shared, q, kv, previous = share(mine, queries, keys, values, prefix_keys, prefix_values)
    return attend(roles, col_count, diagonals, q, kv, previous, shared)


def solution(mesh):
    placed = (
        P(("seq", "head"), None),
        P(("seq", "head"), None),
        P(("seq", "head"), None),
        P("seq", "head"),
        P("seq", "head"),
        P("head"),
        P("head", None),
        P("head"),
        P("head", None),
    )
    return jax.shard_map(
        shards, mesh=mesh, in_specs=placed, out_specs=P("seq", "head"), check_vma=False
    )
```

time: 143 us -> 120 us (0.84)
  Pallas kernels: 128 us -> 111 us
  other arithmetic: 3.3 us -> 0 us
    pallas_call x2 -> x1, Pallas kernels: 50.4 us -> 32.2 us  [attend(): pl.pallas_call(attend_kernel, grid_spec=pltpu.PrefetchScalarGridSpec(num_...]
    gather x4 -> x0, local copies, waits for them, and re-layouts: 1.86 us -> none  [the longest x1 0.66 us: shards(): counts = col_count[finders]]
    reduce_sum x4 -> x0, other arithmetic: 1.8 us -> none  [the longest x1 1.33 us: compact(): used = jnp.sum(flags)]
    unnamed x18 -> x22, local copies, waits for them, and re-layouts: 6.91 us -> 8.22 us
where the time goes in v2:
time: 120 us; the launch traced here: 119 us
  Pallas kernels  111 us (92%)
  local copies, waits for them, and re-layouts  8.22 us (7%)
    pallas_call x1, Pallas kernels, share(): pl.pallas_call(functools.partial(share_kernel, size, heads, orders), out_...  72.6 us
    pallas_call x1, Pallas kernels, attend(): pl.pallas_call(attend_kernel, grid_spec=pltpu.PrefetchScalarGridSpec(num_...  32.2 us
    unnamed x22, local copies, waits for them, and re-layouts  8.22 us
    pallas_call x1, Pallas kernels, collect(): pl.pallas_call(collect_kernel, grid_spec=pltpu.PrefetchScalarGridSpec(num...  6.21 us

profile of v2, /device:TPU:5, one launch (start us, length us, event | category | flops | bytes accessed | tf_op | source)
XLA Modules:
  0.0 119.3 jit_solution(3373727552605206659)
XLA Ops:
  0.0 0.8 copy.10.columns
  0.8 0.8 copy.11.diagonals
  1.5 0.0 copy-start
  1.5 1.6 %copy-done = bf16[2048,512]{1,0:T(8,128)(2,1)S(1)} copy-done((bf16[2048,512]{1,0:T(8,128)(2,1)S(1)}, bf16[2048,512]{1,0:T(8,128)(2,1)}, u32[]{:S(2)}) %copy-start) | copy-done | bytes 2097176
  3.1 0.0 copy-start.2
  3.1 1.6 %copy-done.2 = bf16[2048,512]{1,0:T(8,128)(2,1)S(1)} copy-done((bf16[2048,512]{1,0:T(8,128)(2,1)S(1)}, bf16[2048,512]{1,0:T(8,128)(2,1)}, u32[]{:S(2)}) %copy-start.2) | copy-done | bytes 2097176
  4.7 0.0 copy-start.3
  4.7 0.7 copy-done.3
  5.4 0.0 copy-start.5
  5.4 0.7 copy-done.5
  6.0 0.0 copy-start.1
  6.0 0.0 copy-start.7
  6.0 0.0 copy-start.8
  6.0 6.2 %collect_columns.1.mine = bf16[13312,128]{1,0:T(8,128)(2,1)S(1)} custom-call(s32[1]{0:T(128)} %bitcast.seq, s32[32]{0:T(128)S(1)} %copy-done.3, s32[32,6]{1,0:T(8,128)S(1)} %copy.10.columns, s32[32]{0:T(128)S(1)} %copy-done.5, bf16[2048,512]{1,0:T(8,128)(2,1)S(1)} %copy-done, bf16[2048,512]{1,0:T(8,128)(2,1)S(1)} %copy-done.2), custom_call_target="tpu_custom_call" | custom-call | tf_op jit(solution)/shard_map/collect_columns/pallas_call | solution.py:95
  12.2 0.0 copy-done.1
  12.3 0.0 copy-done.7
  12.3 0.0 copy-done.8
  12.3 0.0 copy-start.4
  12.3 0.0 copy-start.6
  12.3 72.6 %share_columns.1 = (bf16[13312,128]{1,0:T(8,128)(2,1)S(1)}, bf16[512,4096]{1,0:T(8,128)(2,1)}, bf16[512,1024]{1,0:T(8,128)(2,1)S(1)}, bf16[512,1024]{1,0:T(8,128)(2,1)S(1)}) custom-call(bf16[13312,128]{1,0:T(8,128)(2,1)S(1)} %collect_columns.1.mine, bf16[256,8192]{1,0:T(8,128)(2,1)} %queries.1, bf16[256,1024]{1,0:T(8,128)(2,1)S(1)} %copy-done.7, ...), custom_call_target="tpu_custom_call" | custom-call | flops 10000000000 | bytes 13631488 | tf_op jit(solution)/shard_map/share_columns/pallas_call | solution.py:309
  84.9 0.0 copy-done.4
  84.9 0.0 copy-done.6
  84.9 0.0 copy-start.9
  84.9 2.2 %copy-done.9 = bf16[512,4096]{1,0:T(8,128)(2,1)S(1)} copy-done((bf16[512,4096]{1,0:T(8,128)(2,1)S(1)}, bf16[512,4096]{1,0:T(8,128)(2,1)}, u32[]{:S(2)}) %copy-start.9) | copy-done | bytes 4194328
  87.1 32.2 %attend.1 = bf16[512,4096]{1,0:T(8,128)(2,1)} custom-call(s32[32]{0:T(128)S(1)} %copy-done.4, s32[32]{0:T(128)S(1)} %copy-done.6, s32[32,4]{1,0:T(8,128)S(1)} %copy.11.diagonals, bf16[512,4096]{1,0:T(8,128)(2,1)S(1)} %copy-done.9, bf16[512,1024]{1,0:T(8,128)(2,1)S(1)} %get-tuple-element.10.k.v, bf16[512,1024]{1,0:T(8,128)(2,1)S(1)} %get-tuple-element.10.k.v, ...), custom_call_target="tpu_custom_call" | custom-call | flops 12884901888 | bytes 8388608 | tf_op jit(solution)/shard_map/attend/pallas_call | solution.py:467
Async XLA Ops:
  1.5 1.6 %copy-start = (bf16[2048,512]{1,0:T(8,128)(2,1)S(1)}, bf16[2048,512]{1,0:T(8,128)(2,1)}, u32[]{:S(2)}) copy-start(bf16[2048,512]{1,0:T(8,128)(2,1)} %cache_k.1) | copy-start | bytes 6291460
  3.1 1.6 %copy-start.2 = (bf16[2048,512]{1,0:T(8,128)(2,1)S(1)}, bf16[2048,512]{1,0:T(8,128)(2,1)}, u32[]{:S(2)}) copy-start(bf16[2048,512]{1,0:T(8,128)(2,1)} %cache_v.1) | copy-start | bytes 6291460
  4.7 0.7 copy-start.3
  5.4 0.7 copy-start.5
  6.0 6.2 %copy-start.1 = (bf16[2048,512]{1,0:T(8,128)(2,1)S(1)}, bf16[2048,512]{1,0:T(8,128)(2,1)}, u32[]{:S(2)}) copy-start(bf16[2048,512]{1,0:T(8,128)(2,1)} %cache_k.1) | copy-start | bytes 6291460
  6.0 6.2 %copy-start.7 = (bf16[256,1024]{1,0:T(8,128)(2,1)S(1)}, bf16[256,1024]{1,0:T(8,128)(2,1)}, u32[]{:S(2)}) copy-start(bf16[256,1024]{1,0:T(8,128)(2,1)} %keys.1) | copy-start | bytes 1572868
  6.0 6.2 %copy-start.8 = (bf16[256,1024]{1,0:T(8,128)(2,1)S(1)}, bf16[256,1024]{1,0:T(8,128)(2,1)}, u32[]{:S(2)}) copy-start(bf16[256,1024]{1,0:T(8,128)(2,1)} %values.1) | copy-start | bytes 1572868
  12.3 72.6 %copy-start.4 = (s32[32]{0:T(128)S(1)}, s32[32]{0:T(128)}, u32[]{:S(2)}) copy-start(s32[32]{0:T(128)} %roles.3) | copy-start | bytes 388
  12.3 72.6 %copy-start.6 = (s32[32]{0:T(128)S(1)}, s32[32]{0:T(128)}, u32[]{:S(2)}) copy-start(s32[32]{0:T(128)} %col_count.3) | copy-start | bytes 388
  84.9 2.2 %copy-start.9 = (bf16[512,4096]{1,0:T(8,128)(2,1)S(1)}, bf16[512,4096]{1,0:T(8,128)(2,1)}, u32[]{:S(2)}) copy-start(bf16[512,4096]{1,0:T(8,128)(2,1)} %get-tuple-element.9.q) | copy-start | bytes 12582916

commit v3 on v2

--- a/solution.py
+++ b/solution.py
@@ -19,8 +19,9 @@
 NSL = 4
 MAX_RETRIEVERS = 4
 QB = 128
+STREAMS = 4
 SCALE = math.log2(math.e) / math.sqrt(D)
-VMEM_LIMIT = 40 * 1024 * 1024
+VMEM_LIMIT = 58 * 1024 * 1024
 
 
 def dot_nt(a, b):
@@ -299,7 +300,7 @@
 def share(mine, queries, keys, values, prefix_keys, prefix_values):
     size, heads = lax.axis_size("seq"), lax.axis_size("head")
     bits = size.bit_length() - 1
-    orders = [list(range(bits)), [0, *range(2, bits), 1]]
+    orders = [list(range(bits)), [0, *range(2, bits), 1]] * (STREAMS // 2)
     rows = mine.shape[0]
     kind = mine.dtype
     span = keys.shape[0] * heads
@@ -504,7 +505,7 @@
     seq = lax.axis_index("seq").astype(jnp.int32).reshape(1)
     kv_count = prefix_keys.shape[1] // D
     needed = 2 * kv_count * (MAX_RETRIEVERS * VB * BLK + SINK)
-    unit = 2 * 16 * seq_size
+    unit = STREAMS * 16 * seq_size
     rows = -(-needed // unit) * unit
     mine = collect(seq, roles, columns, col_count, prefix_keys, prefix_values, rows)
     shared, q, kv, previous = share(mine, queries, keys, values, prefix_keys, prefix_values)

time: 120 us -> 134 us (1.12)
  the two profiles are of different devices: /device:TPU:5 before, /device:TPU:0 now
where the time goes in v3:
time: 134 us; the launch traced here: 132 us
  Pallas kernels  130 us (97%)
  local copies, waits for them, and re-layouts  2.72 us (2%)
    pallas_call x1, Pallas kernels, share(): pl.pallas_call(functools.partial(share_kernel, size, heads, orders), out_...  90.4 us
    pallas_call x1, Pallas kernels, attend(): pl.pallas_call(attend_kernel, grid_spec=pltpu.PrefetchScalarGridSpec(num_...  32.1 us
    pallas_call x1, Pallas kernels, collect(): pl.pallas_call(collect_kernel, grid_spec=pltpu.PrefetchScalarGridSpec(num...  7.13 us
    unnamed x2, local copies, waits for them, and re-layouts  2.72 us

profile of v3, /device:TPU:0, one launch (start us, length us, event | category | flops | bytes accessed | tf_op | source)
XLA Modules:
  0.0 132.3 jit_solution(1761997510865620651)
XLA Ops:
  0.0 1.4 %copy.10.columns = s32[32,6]{1,0:T(8,128)} copy(s32[32,6]{0,1:T(8,128)} %param.15) | data formatting | bytes 1536 | tf_op args[6]
  1.4 1.4 %copy.11.diagonals = s32[32,4]{1,0:T(8,128)} copy(s32[32,4]{0,1:T(4,128)} %param.17) | data formatting | bytes 1024 | tf_op args[8]
  2.7 7.1 %collect_columns.1.mine = bf16[13312,128]{1,0:T(8,128)(2,1)} custom-call(s32[1]{0:T(128)} %bitcast.seq, s32[32]{0:T(128)} %roles.3, s32[32,6]{1,0:T(8,128)} %copy.10.columns, s32[32]{0:T(128)} %col_count.3, bf16[2048,512]{1,0:T(8,128)(2,1)} %cache_k.1, bf16[2048,512]{1,0:T(8,128)(2,1)} %cache_v.1), custom_call_target="tpu_custom_call" | custom-call | tf_op jit(solution)/shard_map/collect_columns/pallas_call | solution.py:96
  9.9 90.4 %share_columns.1 = (bf16[13312,128]{1,0:T(8,128)(2,1)}, bf16[512,4096]{1,0:T(8,128)(2,1)}, bf16[512,1024]{1,0:T(8,128)(2,1)}, bf16[512,1024]{1,0:T(8,128)(2,1)}) custom-call(bf16[13312,128]{1,0:T(8,128)(2,1)} %collect_columns.1.mine, bf16[256,8192]{1,0:T(8,128)(2,1)} %queries.1, bf16[256,1024]{1,0:T(8,128)(2,1)} %keys.1, bf16[256,1024]{1,0:T(8,128)(2,1)} %values.1, ...), custom_call_target="tpu_custom_call" | custom-call | flops 10000000000 | bytes 13631488 | tf_op jit(solution)/shard_map/share_columns/pallas_call | solution.py:310
  100.2 32.1 %attend.1 = bf16[512,4096]{1,0:T(8,128)(2,1)} custom-call(s32[32]{0:T(128)} %roles.3, s32[32]{0:T(128)} %col_count.3, s32[32,4]{1,0:T(8,128)} %copy.11.diagonals, bf16[512,4096]{1,0:T(8,128)(2,1)} %get-tuple-element.9.q, bf16[512,1024]{1,0:T(8,128)(2,1)} %get-tuple-element.10.k.v, bf16[512,1024]{1,0:T(8,128)(2,1)} %get-tuple-element.10.k.v, ...), custom_call_target="tpu_custom_call" | custom-call | flops 12884901888 | bytes 8388608 | tf_op jit(solution)/shard_map/attend/pallas_call | solution.py:468

commit v4 on v2

--- a/solution.py
+++ b/solution.py
@@ -288,7 +288,7 @@
                 halve(w, step)
             elif step < 2 * bits:
                 double(w, step)
-        if step == 1:
+        if step == bits - 1:
             pass_tails()
     for copy in tails(False):
         copy.wait()
@@ -299,7 +299,7 @@
 def share(mine, queries, keys, values, prefix_keys, prefix_values):
     size, heads = lax.axis_size("seq"), lax.axis_size("head")
     bits = size.bit_length() - 1
-    orders = [list(range(bits)), [0, *range(2, bits), 1]]
+    orders = [list(range(bits)), [0, 2, 1, *range(3, bits)]]
     rows = mine.shape[0]
     kind = mine.dtype
     span = keys.shape[0] * heads
@@ -388,11 +388,18 @@
         pair = [lanes(passers[2 * t]), lanes(passers[2 * t + 1])]
         row = lax.rem(lax.broadcasted_iota(jnp.int32, (2 * QB, QB), 0), QB)
         col = lax.broadcasted_iota(jnp.int32, (2 * QB, QB), 1)
-        for r in range(0, rows, QB):
+
+        def scores(r):
             low, high = SINK + r, SINK + r + WIN + QB
             q_rows = jnp.concatenate([q[r : r + QB, place] for place in pair], 0)
-            window = jnp.concatenate([keys_t[:, :SINK], keys_t[:, low:high]], 1)
-            s = dot(q_rows, window)
+            return dot(q_rows, jnp.concatenate([keys_t[:, :SINK], keys_t[:, low:high]], 1))
+
+        ahead = scores(0)
+        for r in range(0, rows, QB):
+            s = ahead
+            if r + QB < rows:
+                ahead = scores(r + QB)
+            low, high = SINK + r, SINK + r + WIN + QB
             s = jnp.concatenate(
                 [
                     s[:, :SINK],
@@ -430,13 +437,22 @@
             q_head = q[:, lanes(i)]
             s_vert = jnp.where(open_cols, dot_nt(q_head, far_k[place, :]), -jnp.inf)
             p_verts, slashes = [], []
-            for r in range(0, rows, BLK):
-                starts = [
+
+            def starts(r):
+                return [
                     pl.multiple_of(WIN + r - diagonals[head, t] * BLK, BLK) for t in range(NSL)
                 ]
-                near_k = jnp.concatenate([keys[pl.ds(at, BLK), :] for at in starts], 0)
-                near_v = jnp.concatenate([vals[pl.ds(SINK + at, BLK), :] for at in starts], 0)
-                s_near = jnp.where(causal, dot_nt(q_head[r : r + BLK], near_k), -jnp.inf)
+
+            def scores(r):
+                near_k = jnp.concatenate([keys[pl.ds(at, BLK), :] for at in starts(r)], 0)
+                return dot_nt(q_head[r : r + BLK], near_k)
+
+            nears = [scores(r) for r in range(0, rows, BLK)]
+            for r in range(0, rows, BLK):
+                near_v = jnp.concatenate(
+                    [vals[pl.ds(SINK + at, BLK), :] for at in starts(r)], 0
+                )
+                s_near = jnp.where(causal, nears[r // BLK], -jnp.inf)
                 s_far = s_vert[r : r + BLK]
                 top = jnp.maximum(
                     jnp.max(s_near, axis=1, keepdims=True), jnp.max(s_far, axis=1, keepdims=True)

time: 120 us -> 117 us (0.975)
  Pallas kernels: 111 us -> 109 us
    pallas_call x1, Pallas kernels: 32.2 us -> 28.9 us  [attend(): pl.pallas_call(attend_kernel, grid_spec=pltpu.PrefetchScalarGridSpec(num_...]
    pallas_call x1, Pallas kernels: 72.6 us -> 74 us  [share(): pl.pallas_call(functools.partial(share_kernel, size, heads, orders), out_...]
where the time goes in v4:
time: 117 us
  Pallas kernels  109 us (93%)
  local copies, waits for them, and re-layouts  8.22 us (7%)
    pallas_call x1, Pallas kernels, share(): pl.pallas_call(functools.partial(share_kernel, size, heads, orders), out_...  74 us
    pallas_call x1, Pallas kernels, attend(): pl.pallas_call(attend_kernel, grid_spec=pltpu.PrefetchScalarGridSpec(num_...  28.9 us
    unnamed x22, local copies, waits for them, and re-layouts  8.22 us
    pallas_call x1, Pallas kernels, collect(): pl.pallas_call(collect_kernel, grid_spec=pltpu.PrefetchScalarGridSpec(num...  6.07 us

profile of v4, /device:TPU:5, one launch (start us, length us, event | category | flops | bytes accessed | tf_op | source)
XLA Modules:
  0.0 117.3 jit_solution(2834041963910631138)
XLA Ops:
  0.0 0.8 copy.10.columns
  0.8 0.8 copy.11.diagonals
  1.5 0.0 copy-start
  1.5 1.6 %copy-done = bf16[2048,512]{1,0:T(8,128)(2,1)S(1)} copy-done((bf16[2048,512]{1,0:T(8,128)(2,1)S(1)}, bf16[2048,512]{1,0:T(8,128)(2,1)}, u32[]{:S(2)}) %copy-start) | copy-done | bytes 2097176
  3.1 0.0 copy-start.2
  3.1 1.6 %copy-done.2 = bf16[2048,512]{1,0:T(8,128)(2,1)S(1)} copy-done((bf16[2048,512]{1,0:T(8,128)(2,1)S(1)}, bf16[2048,512]{1,0:T(8,128)(2,1)}, u32[]{:S(2)}) %copy-start.2) | copy-done | bytes 2097176
  4.7 0.0 copy-start.3
  4.7 0.7 copy-done.3
  5.4 0.0 copy-start.5
  5.4 0.7 copy-done.5
  6.0 0.0 copy-start.1
  6.0 0.0 copy-start.7
  6.0 0.0 copy-start.8
  6.0 6.1 %collect_columns.1.mine = bf16[13312,128]{1,0:T(8,128)(2,1)S(1)} custom-call(s32[1]{0:T(128)} %bitcast.seq, s32[32]{0:T(128)S(1)} %copy-done.3, s32[32,6]{1,0:T(8,128)S(1)} %copy.10.columns, s32[32]{0:T(128)S(1)} %copy-done.5, bf16[2048,512]{1,0:T(8,128)(2,1)S(1)} %copy-done, bf16[2048,512]{1,0:T(8,128)(2,1)S(1)} %copy-done.2), custom_call_target="tpu_custom_call" | custom-call | tf_op jit(solution)/shard_map/collect_columns/pallas_call | solution.py:95
  12.1 0.0 copy-done.1
  12.1 0.0 copy-done.7
  12.1 0.0 copy-done.8
  12.1 0.0 copy-start.4
  12.2 0.0 copy-start.6
  12.2 74.0 %share_columns.1 = (bf16[13312,128]{1,0:T(8,128)(2,1)S(1)}, bf16[512,4096]{1,0:T(8,128)(2,1)}, bf16[512,1024]{1,0:T(8,128)(2,1)S(1)}, bf16[512,1024]{1,0:T(8,128)(2,1)S(1)}) custom-call(bf16[13312,128]{1,0:T(8,128)(2,1)S(1)} %collect_columns.1.mine, bf16[256,8192]{1,0:T(8,128)(2,1)} %queries.1, bf16[256,1024]{1,0:T(8,128)(2,1)S(1)} %copy-done.7, ...), custom_call_target="tpu_custom_call" | custom-call | flops 10000000000 | bytes 13631488 | tf_op jit(solution)/shard_map/share_columns/pallas_call | solution.py:309
  86.1 0.0 copy-done.4
  86.1 0.0 copy-done.6
  86.1 0.0 copy-start.9
  86.2 2.2 %copy-done.9 = bf16[512,4096]{1,0:T(8,128)(2,1)S(1)} copy-done((bf16[512,4096]{1,0:T(8,128)(2,1)S(1)}, bf16[512,4096]{1,0:T(8,128)(2,1)}, u32[]{:S(2)}) %copy-start.9) | copy-done | bytes 4194328
  88.3 28.9 %attend.1 = bf16[512,4096]{1,0:T(8,128)(2,1)} custom-call(s32[32]{0:T(128)S(1)} %copy-done.4, s32[32]{0:T(128)S(1)} %copy-done.6, s32[32,4]{1,0:T(8,128)S(1)} %copy.11.diagonals, bf16[512,4096]{1,0:T(8,128)(2,1)S(1)} %copy-done.9, bf16[512,1024]{1,0:T(8,128)(2,1)S(1)} %get-tuple-element.10.k.v, bf16[512,1024]{1,0:T(8,128)(2,1)S(1)} %get-tuple-element.10.k.v, ...), custom_call_target="tpu_custom_call" | custom-call | flops 12884901888 | bytes 8388608 | tf_op jit(solution)/shard_map/attend/pallas_call | solution.py:483
Async XLA Ops:
  1.5 1.6 %copy-start = (bf16[2048,512]{1,0:T(8,128)(2,1)S(1)}, bf16[2048,512]{1,0:T(8,128)(2,1)}, u32[]{:S(2)}) copy-start(bf16[2048,512]{1,0:T(8,128)(2,1)} %cache_k.1) | copy-start | bytes 6291460
  3.1 1.6 %copy-start.2 = (bf16[2048,512]{1,0:T(8,128)(2,1)S(1)}, bf16[2048,512]{1,0:T(8,128)(2,1)}, u32[]{:S(2)}) copy-start(bf16[2048,512]{1,0:T(8,128)(2,1)} %cache_v.1) | copy-start | bytes 6291460
  4.7 0.7 copy-start.3
  5.4 0.7 copy-start.5
  6.0 6.1 %copy-start.1 = (bf16[2048,512]{1,0:T(8,128)(2,1)S(1)}, bf16[2048,512]{1,0:T(8,128)(2,1)}, u32[]{:S(2)}) copy-start(bf16[2048,512]{1,0:T(8,128)(2,1)} %cache_k.1) | copy-start | bytes 6291460
  6.0 6.1 %copy-start.7 = (bf16[256,1024]{1,0:T(8,128)(2,1)S(1)}, bf16[256,1024]{1,0:T(8,128)(2,1)}, u32[]{:S(2)}) copy-start(bf16[256,1024]{1,0:T(8,128)(2,1)} %keys.1) | copy-start | bytes 1572868
  6.0 6.1 %copy-start.8 = (bf16[256,1024]{1,0:T(8,128)(2,1)S(1)}, bf16[256,1024]{1,0:T(8,128)(2,1)}, u32[]{:S(2)}) copy-start(bf16[256,1024]{1,0:T(8,128)(2,1)} %values.1) | copy-start | bytes 1572868
  12.1 74.0 %copy-start.4 = (s32[32]{0:T(128)S(1)}, s32[32]{0:T(128)}, u32[]{:S(2)}) copy-start(s32[32]{0:T(128)} %roles.3) | copy-start | bytes 388
  12.2 74.0 %copy-start.6 = (s32[32]{0:T(128)S(1)}, s32[32]{0:T(128)}, u32[]{:S(2)}) copy-start(s32[32]{0:T(128)} %col_count.3) | copy-start | bytes 388
  86.1 2.2 %copy-start.9 = (bf16[512,4096]{1,0:T(8,128)(2,1)S(1)}, bf16[512,4096]{1,0:T(8,128)(2,1)}, u32[]{:S(2)}) copy-start(bf16[512,4096]{1,0:T(8,128)(2,1)} %get-tuple-element.9.q) | copy-start | bytes 12582916

commit v5 on v4

--- a/solution.py
+++ b/solution.py
@@ -288,7 +288,7 @@
                 halve(w, step)
             elif step < 2 * bits:
                 double(w, step)
-        if step == bits - 1:
+        if step == 1:
             pass_tails()
     for copy in tails(False):
         copy.wait()
@@ -299,7 +299,7 @@
 def share(mine, queries, keys, values, prefix_keys, prefix_values):
     size, heads = lax.axis_size("seq"), lax.axis_size("head")
     bits = size.bit_length() - 1
-    orders = [list(range(bits)), [0, 2, 1, *range(3, bits)]]
+    orders = [list(range(bits)), [0, *range(2, bits), 1]]
     rows = mine.shape[0]
     kind = mine.dtype
     span = keys.shape[0] * heads

time: 117 us -> 117 us (level)
  the two profiles are of different devices: /device:TPU:5 before, /device:TPU:11 now
where the time goes in v5:
time: 117 us; the launch traced here: 115 us
  Pallas kernels  107 us (91%)
  local copies, waits for them, and re-layouts  8.22 us (7%)
    pallas_call x1, Pallas kernels, share(): pl.pallas_call(functools.partial(share_kernel, size, heads, orders), out_...  72 us
    pallas_call x1, Pallas kernels, attend(): pl.pallas_call(attend_kernel, grid_spec=pltpu.PrefetchScalarGridSpec(num_...  29.1 us
    unnamed x22, local copies, waits for them, and re-layouts  8.22 us
    pallas_call x1, Pallas kernels, collect(): pl.pallas_call(collect_kernel, grid_spec=pltpu.PrefetchScalarGridSpec(num...  5.52 us

profile of v5, /device:TPU:11, one launch (start us, length us, event | category | flops | bytes accessed | tf_op | source)
XLA Modules:
  0.0 114.9 jit_solution(3531291919508244602)
XLA Ops:
  0.0 0.8 copy.10.columns
  0.8 0.8 copy.11.diagonals
  1.5 0.0 copy-start
  1.5 1.6 %copy-done = bf16[2048,512]{1,0:T(8,128)(2,1)S(1)} copy-done((bf16[2048,512]{1,0:T(8,128)(2,1)S(1)}, bf16[2048,512]{1,0:T(8,128)(2,1)}, u32[]{:S(2)}) %copy-start) | copy-done | bytes 2097176
  3.1 0.0 copy-start.2
  3.1 1.6 %copy-done.2 = bf16[2048,512]{1,0:T(8,128)(2,1)S(1)} copy-done((bf16[2048,512]{1,0:T(8,128)(2,1)S(1)}, bf16[2048,512]{1,0:T(8,128)(2,1)}, u32[]{:S(2)}) %copy-start.2) | copy-done | bytes 2097176
  4.7 0.0 copy-start.3
  4.7 0.7 copy-done.3
  5.4 0.0 copy-start.5
  5.4 0.7 copy-done.5
  6.0 0.0 copy-start.1
  6.0 0.0 copy-start.7
  6.0 0.0 copy-start.8
  6.0 5.5 %collect_columns.1.mine = bf16[13312,128]{1,0:T(8,128)(2,1)S(1)} custom-call(s32[1]{0:T(128)} %bitcast.seq, s32[32]{0:T(128)S(1)} %copy-done.3, s32[32,6]{1,0:T(8,128)S(1)} %copy.10.columns, s32[32]{0:T(128)S(1)} %copy-done.5, bf16[2048,512]{1,0:T(8,128)(2,1)S(1)} %copy-done, bf16[2048,512]{1,0:T(8,128)(2,1)S(1)} %copy-done.2), custom_call_target="tpu_custom_call" | custom-call | tf_op jit(solution)/shard_map/collect_columns/pallas_call | solution.py:95
  11.6 0.0 copy-done.1
  11.6 0.0 copy-done.7
  11.6 0.0 copy-done.8
  11.6 0.0 copy-start.4
  11.6 0.0 copy-start.6
  11.6 72.0 %share_columns.1 = (bf16[13312,128]{1,0:T(8,128)(2,1)S(1)}, bf16[512,4096]{1,0:T(8,128)(2,1)}, bf16[512,1024]{1,0:T(8,128)(2,1)S(1)}, bf16[512,1024]{1,0:T(8,128)(2,1)S(1)}) custom-call(bf16[13312,128]{1,0:T(8,128)(2,1)S(1)} %collect_columns.1.mine, bf16[256,8192]{1,0:T(8,128)(2,1)} %queries.1, bf16[256,1024]{1,0:T(8,128)(2,1)S(1)} %copy-done.7, ...), custom_call_target="tpu_custom_call" | custom-call | flops 10000000000 | bytes 13631488 | tf_op jit(solution)/shard_map/share_columns/pallas_call | solution.py:309
  83.6 0.0 copy-done.4
  83.6 0.0 copy-done.6
  83.6 0.0 copy-start.9
  83.6 2.2 %copy-done.9 = bf16[512,4096]{1,0:T(8,128)(2,1)S(1)} copy-done((bf16[512,4096]{1,0:T(8,128)(2,1)S(1)}, bf16[512,4096]{1,0:T(8,128)(2,1)}, u32[]{:S(2)}) %copy-start.9) | copy-done | bytes 4194328
  85.8 29.1 %attend.1 = bf16[512,4096]{1,0:T(8,128)(2,1)} custom-call(s32[32]{0:T(128)S(1)} %copy-done.4, s32[32]{0:T(128)S(1)} %copy-done.6, s32[32,4]{1,0:T(8,128)S(1)} %copy.11.diagonals, bf16[512,4096]{1,0:T(8,128)(2,1)S(1)} %copy-done.9, bf16[512,1024]{1,0:T(8,128)(2,1)S(1)} %get-tuple-element.10.k.v, bf16[512,1024]{1,0:T(8,128)(2,1)S(1)} %get-tuple-element.10.k.v, ...), custom_call_target="tpu_custom_call" | custom-call | flops 12884901888 | bytes 8388608 | tf_op jit(solution)/shard_map/attend/pallas_call | solution.py:483
Async XLA Ops:
  1.5 1.6 %copy-start = (bf16[2048,512]{1,0:T(8,128)(2,1)S(1)}, bf16[2048,512]{1,0:T(8,128)(2,1)}, u32[]{:S(2)}) copy-start(bf16[2048,512]{1,0:T(8,128)(2,1)} %cache_k.1) | copy-start | bytes 6291460
  3.1 1.6 %copy-start.2 = (bf16[2048,512]{1,0:T(8,128)(2,1)S(1)}, bf16[2048,512]{1,0:T(8,128)(2,1)}, u32[]{:S(2)}) copy-start(bf16[2048,512]{1,0:T(8,128)(2,1)} %cache_v.1) | copy-start | bytes 6291460
  4.7 0.7 copy-start.3
  5.4 0.7 copy-start.5
  6.0 5.5 %copy-start.1 = (bf16[2048,512]{1,0:T(8,128)(2,1)S(1)}, bf16[2048,512]{1,0:T(8,128)(2,1)}, u32[]{:S(2)}) copy-start(bf16[2048,512]{1,0:T(8,128)(2,1)} %cache_k.1) | copy-start | bytes 6291460
  6.0 5.5 %copy-start.7 = (bf16[256,1024]{1,0:T(8,128)(2,1)S(1)}, bf16[256,1024]{1,0:T(8,128)(2,1)}, u32[]{:S(2)}) copy-start(bf16[256,1024]{1,0:T(8,128)(2,1)} %keys.1) | copy-start | bytes 1572868
  6.0 5.6 %copy-start.8 = (bf16[256,1024]{1,0:T(8,128)(2,1)S(1)}, bf16[256,1024]{1,0:T(8,128)(2,1)}, u32[]{:S(2)}) copy-start(bf16[256,1024]{1,0:T(8,128)(2,1)} %values.1) | copy-start | bytes 1572868
  11.6 72.0 %copy-start.4 = (s32[32]{0:T(128)S(1)}, s32[32]{0:T(128)}, u32[]{:S(2)}) copy-start(s32[32]{0:T(128)} %roles.3) | copy-start | bytes 388
  11.6 72.0 %copy-start.6 = (s32[32]{0:T(128)S(1)}, s32[32]{0:T(128)}, u32[]{:S(2)}) copy-start(s32[32]{0:T(128)} %col_count.3) | copy-start | bytes 388
  83.6 2.2 %copy-start.9 = (bf16[512,4096]{1,0:T(8,128)(2,1)S(1)}, bf16[512,4096]{1,0:T(8,128)(2,1)}, u32[]{:S(2)}) copy-start(bf16[512,4096]{1,0:T(8,128)(2,1)} %get-tuple-element.9.q) | copy-start | bytes 12582916

commit v6 on v5

--- a/solution.py
+++ b/solution.py
@@ -299,7 +299,7 @@
 def share(mine, queries, keys, values, prefix_keys, prefix_values):
     size, heads = lax.axis_size("seq"), lax.axis_size("head")
     bits = size.bit_length() - 1
-    orders = [list(range(bits)), [0, *range(2, bits), 1]]
+    orders = [list(range(bits)), [0, 2, 1, *range(3, bits)]]
     rows = mine.shape[0]
     kind = mine.dtype
     span = keys.shape[0] * heads

time: 117 us -> 118 us (level)
  the two profiles are of different devices: /device:TPU:11 before, /device:TPU:5 now
where the time goes in v6:
time: 118 us; the launch traced here: 117 us
  Pallas kernels  109 us (92%)
  local copies, waits for them, and re-layouts  8.22 us (7%)
    pallas_call x1, Pallas kernels, share(): pl.pallas_call(functools.partial(share_kernel, size, heads, orders), out_...  74.2 us
    pallas_call x1, Pallas kernels, attend(): pl.pallas_call(attend_kernel, grid_spec=pltpu.PrefetchScalarGridSpec(num_...  28.9 us
    unnamed x22, local copies, waits for them, and re-layouts  8.22 us
    pallas_call x1, Pallas kernels, collect(): pl.pallas_call(collect_kernel, grid_spec=pltpu.PrefetchScalarGridSpec(num...  6.04 us

profile of v6, /device:TPU:5, one launch (start us, length us, event | category | flops | bytes accessed | tf_op | source)
XLA Modules:
  0.0 117.5 jit_solution(15765879622402055778)
XLA Ops:
  0.0 0.8 copy.10.columns
  0.8 0.8 copy.11.diagonals
  1.5 0.0 copy-start
  1.5 1.6 %copy-done = bf16[2048,512]{1,0:T(8,128)(2,1)S(1)} copy-done((bf16[2048,512]{1,0:T(8,128)(2,1)S(1)}, bf16[2048,512]{1,0:T(8,128)(2,1)}, u32[]{:S(2)}) %copy-start) | copy-done | bytes 2097176
  3.1 0.0 copy-start.2
  3.1 1.6 %copy-done.2 = bf16[2048,512]{1,0:T(8,128)(2,1)S(1)} copy-done((bf16[2048,512]{1,0:T(8,128)(2,1)S(1)}, bf16[2048,512]{1,0:T(8,128)(2,1)}, u32[]{:S(2)}) %copy-start.2) | copy-done | bytes 2097176
  4.7 0.0 copy-start.3
  4.7 0.7 copy-done.3
  5.4 0.0 copy-start.5
  5.4 0.7 copy-done.5
  6.0 0.0 copy-start.1
  6.0 0.0 copy-start.7
  6.0 0.0 copy-start.8
  6.0 6.0 %collect_columns.1.mine = bf16[13312,128]{1,0:T(8,128)(2,1)S(1)} custom-call(s32[1]{0:T(128)} %bitcast.seq, s32[32]{0:T(128)S(1)} %copy-done.3, s32[32,6]{1,0:T(8,128)S(1)} %copy.10.columns, s32[32]{0:T(128)S(1)} %copy-done.5, bf16[2048,512]{1,0:T(8,128)(2,1)S(1)} %copy-done, bf16[2048,512]{1,0:T(8,128)(2,1)S(1)} %copy-done.2), custom_call_target="tpu_custom_call" | custom-call | tf_op jit(solution)/shard_map/collect_columns/pallas_call | solution.py:95
  12.1 0.0 copy-done.1
  12.1 0.0 copy-done.7
  12.1 0.0 copy-done.8
  12.1 0.0 copy-start.4
  12.1 0.0 copy-start.6
  12.1 74.2 %share_columns.1 = (bf16[13312,128]{1,0:T(8,128)(2,1)S(1)}, bf16[512,4096]{1,0:T(8,128)(2,1)}, bf16[512,1024]{1,0:T(8,128)(2,1)S(1)}, bf16[512,1024]{1,0:T(8,128)(2,1)S(1)}) custom-call(bf16[13312,128]{1,0:T(8,128)(2,1)S(1)} %collect_columns.1.mine, bf16[256,8192]{1,0:T(8,128)(2,1)} %queries.1, bf16[256,1024]{1,0:T(8,128)(2,1)S(1)} %copy-done.7, ...), custom_call_target="tpu_custom_call" | custom-call | flops 10000000000 | bytes 13631488 | tf_op jit(solution)/shard_map/share_columns/pallas_call | solution.py:309
  86.4 0.0 copy-done.4
  86.4 0.0 copy-done.6
  86.4 0.0 copy-start.9
  86.4 2.2 %copy-done.9 = bf16[512,4096]{1,0:T(8,128)(2,1)S(1)} copy-done((bf16[512,4096]{1,0:T(8,128)(2,1)S(1)}, bf16[512,4096]{1,0:T(8,128)(2,1)}, u32[]{:S(2)}) %copy-start.9) | copy-done | bytes 4194328
  88.6 28.9 %attend.1 = bf16[512,4096]{1,0:T(8,128)(2,1)} custom-call(s32[32]{0:T(128)S(1)} %copy-done.4, s32[32]{0:T(128)S(1)} %copy-done.6, s32[32,4]{1,0:T(8,128)S(1)} %copy.11.diagonals, bf16[512,4096]{1,0:T(8,128)(2,1)S(1)} %copy-done.9, bf16[512,1024]{1,0:T(8,128)(2,1)S(1)} %get-tuple-element.10.k.v, bf16[512,1024]{1,0:T(8,128)(2,1)S(1)} %get-tuple-element.10.k.v, ...), custom_call_target="tpu_custom_call" | custom-call | flops 12884901888 | bytes 8388608 | tf_op jit(solution)/shard_map/attend/pallas_call | solution.py:483
Async XLA Ops:
  1.5 1.6 %copy-start = (bf16[2048,512]{1,0:T(8,128)(2,1)S(1)}, bf16[2048,512]{1,0:T(8,128)(2,1)}, u32[]{:S(2)}) copy-start(bf16[2048,512]{1,0:T(8,128)(2,1)} %cache_k.1) | copy-start | bytes 6291460
  3.1 1.6 %copy-start.2 = (bf16[2048,512]{1,0:T(8,128)(2,1)S(1)}, bf16[2048,512]{1,0:T(8,128)(2,1)}, u32[]{:S(2)}) copy-start(bf16[2048,512]{1,0:T(8,128)(2,1)} %cache_v.1) | copy-start | bytes 6291460
  4.7 0.7 copy-start.3
  5.4 0.7 copy-start.5
  6.0 6.1 %copy-start.1 = (bf16[2048,512]{1,0:T(8,128)(2,1)S(1)}, bf16[2048,512]{1,0:T(8,128)(2,1)}, u32[]{:S(2)}) copy-start(bf16[2048,512]{1,0:T(8,128)(2,1)} %cache_k.1) | copy-start | bytes 6291460
  6.0 6.1 %copy-start.7 = (bf16[256,1024]{1,0:T(8,128)(2,1)S(1)}, bf16[256,1024]{1,0:T(8,128)(2,1)}, u32[]{:S(2)}) copy-start(bf16[256,1024]{1,0:T(8,128)(2,1)} %keys.1) | copy-start | bytes 1572868
  6.0 6.1 %copy-start.8 = (bf16[256,1024]{1,0:T(8,128)(2,1)S(1)}, bf16[256,1024]{1,0:T(8,128)(2,1)}, u32[]{:S(2)}) copy-start(bf16[256,1024]{1,0:T(8,128)(2,1)} %values.1) | copy-start | bytes 1572868
  12.1 74.3 %copy-start.4 = (s32[32]{0:T(128)S(1)}, s32[32]{0:T(128)}, u32[]{:S(2)}) copy-start(s32[32]{0:T(128)} %roles.3) | copy-start | bytes 388
  12.1 74.3 %copy-start.6 = (s32[32]{0:T(128)S(1)}, s32[32]{0:T(128)}, u32[]{:S(2)}) copy-start(s32[32]{0:T(128)} %col_count.3) | copy-start | bytes 388
  86.4 2.2 %copy-start.9 = (bf16[512,4096]{1,0:T(8,128)(2,1)S(1)}, bf16[512,4096]{1,0:T(8,128)(2,1)}, u32[]{:S(2)}) copy-start(bf16[512,4096]{1,0:T(8,128)(2,1)} %get-tuple-element.9.q) | copy-start | bytes 12582916
